TPU v7x, 32 devices: a whole 2x2x4 slice. The times are simulated.
32 devices in a mesh: grp: 2 (over y), fsdp: 4 (over z), rows: 4 (over x, core).
Axes of the slice: x: 2, y: 2, z: 4, core: 2. Of those that a mesh axis runs over, the one named last changes fastest.
Arguments:
- rollout: bfloat16 [4096, 8192], P(('grp', 'fsdp', 'rows')), parts along dimension 0, may hold values from -6 to 6
- row_adapter_index: int32 [4096, 1], P(('grp', 'fsdp', 'rows')), parts along dimension 0, may hold values from 0 to 15; in each aligned block of 128 rows (0 to 127, 128 to 255, ...) at most 16 rows name the same one
- frozen_key_weight: bfloat16 [8192, 1024], P('fsdp'), may hold values from -0.0625 to 0.0625
- adapter_down_weight: bfloat16 [32, 8192, 64], P(('grp', 'fsdp', 'rows')), parts along dimension 0, may hold values from -0.0625 to 0.0625
- adapter_up_weight: bfloat16 [32, 64, 1024], P(('grp', 'fsdp', 'rows')), parts along dimension 0, may hold values from -0.75 to 0.75
- output_gradient: bfloat16 [4096, 1024], P(('grp', 'fsdp', 'rows')), parts along dimension 0, may hold values from -6 to 6
Outputs:
- mixed: bfloat16 [4096, 1024], P(('grp', 'fsdp', 'rows')), parts along dimension 0
- grad_down: float32 [32, 8192, 64], P(('grp', 'fsdp', 'rows')), parts along dimension 0
- up_matrix_gradient: float32 [32, 64, 1024], P(('grp', 'fsdp', 'rows')), parts along dimension 0
There are 2 independent parts, one for each index of `grp`. A program takes and returns all parts, laid end to end along the dimension named above; an argument that names none is the same for every part. Nothing has to cross between parts.
Inputs may be any that keep to these rules, and one draw needn't show every extreme that they name: `row_adapter_index`: in each aligned block of 128 rows (the rows of one device) no adapter is named by more than 16 rows, a bound that some block reaches.
All inputs are finite; a program needn't handle non-finite values.
Results may differ from a plain program's by a relative error of at most 0.0045.
Values may be sent and summed in bfloat16 or wider, within the bound.
No kernel may reach another device: no remote copies, remote signals or barrier semaphores. Data moves between devices by JAX's collectives and lax.ppermute only.
A program may use at most 128 MiB of HBM per device.

v0:
```python
import jax
import jax.numpy as jnp
from jax import lax
from jax.sharding import PartitionSpec as P

adapter_scale = 0.5


def per_device(
    rollout,
    row_adapter_index,
    frozen_key_weight,
    adapter_down_weight,
    adapter_up_weight,
    output_gradient,
):
    count, width = rollout.shape
    layer_outputs = frozen_key_weight.shape[1]
    n_fsdp = lax.axis_size("fsdp")
    n_rows = lax.axis_size("rows")
    owner_devices = n_fsdp * n_rows
    slot_positions = 2 * count // owner_devices
    frozen_output = jnp.dot(
        rollout,
        lax.all_gather(frozen_key_weight, "fsdp", axis=0, tiled=True),
        preferred_element_type=jnp.float32,
    )
    ids = row_adapter_index[:, 0]
    onehot = (ids[:, None] == jnp.arange(owner_devices, dtype=jnp.int32)[None, :]).astype(jnp.int32)
    earlier = jnp.cumsum(onehot, 0) - onehot
    position = jnp.sum(earlier * onehot, 1)
    target_adapter = ids * slot_positions + position
    send_x = (
        jnp.zeros((owner_devices * slot_positions, width), jnp.bfloat16)
        .at[target_adapter]
        .set(rollout)
    )
    send_dy = (
        jnp.zeros((owner_devices * slot_positions, layer_outputs), jnp.bfloat16)
        .at[target_adapter]
        .set(output_gradient)
    )
    got_x, got_dy = (
        lax.all_to_all(
            send_x.reshape(owner_devices, slot_positions, width),
            ("fsdp", "rows"),
            split_axis=0,
            concat_axis=0,
            tiled=True,
        ),
        lax.all_to_all(
            send_dy.reshape(owner_devices, slot_positions, layer_outputs),
            ("fsdp", "rows"),
            split_axis=0,
            concat_axis=0,
            tiled=True,
        ),
    )
    flat_x = got_x.reshape(owner_devices * slot_positions, width)
    flat_dy = got_dy.reshape(owner_devices * slot_positions, layer_outputs)
    down_matrix = adapter_down_weight[0]
    up_matrix = adapter_up_weight[0]
    hidden_state = jnp.dot(flat_x, down_matrix, preferred_element_type=jnp.float32).astype(
        jnp.bfloat16
    )
    adapter_term = (
        adapter_scale * jnp.dot(hidden_state, up_matrix, preferred_element_type=jnp.float32)
    ).astype(jnp.bfloat16)
    returned_rows = (
        adapter_scale
        * lax.dot_general(
            flat_dy, up_matrix, (((1,), (1,)), ((), ())), preferred_element_type=jnp.float32
        )
    ).astype(jnp.bfloat16)
    up_matrix_gradient = adapter_scale * lax.dot_general(
        hidden_state, flat_dy, (((0,), (0,)), ((), ())), preferred_element_type=jnp.float32
    )
    grad_down = lax.dot_general(
        flat_x, returned_rows, (((0,), (0,)), ((), ())), preferred_element_type=jnp.float32
    )
    received_rows = lax.all_to_all(
        adapter_term.reshape(owner_devices, slot_positions, layer_outputs),
        ("fsdp", "rows"),
        split_axis=0,
        concat_axis=0,
        tiled=True,
    )
    adapter_row_output = received_rows.reshape(owner_devices * slot_positions, layer_outputs)[
        target_adapter
    ]
    mixed = (frozen_output + adapter_row_output.astype(jnp.float32)).astype(jnp.bfloat16)
    return (mixed, grad_down[None], up_matrix_gradient[None])


def solution(mesh):
    return jax.shard_map(
        per_device,
        mesh=mesh,
        in_specs=(
            P(("grp", "fsdp", "rows"), None),
            P(("grp", "fsdp", "rows"), None),
            P("fsdp", None),
            P(("grp", "fsdp", "rows"), None, None),
            P(("grp", "fsdp", "rows"), None, None),
            P(("grp", "fsdp", "rows"), None),
        ),
        out_specs=(
            P(("grp", "fsdp", "rows"), None),
            P(("grp", "fsdp", "rows"), None, None),
            P(("grp", "fsdp", "rows"), None, None),
        ),
        check_vma=False,
    )
```

profile of v0, /device:TPU:0, one launch (start us, length us, event | category | flops | bytes accessed | tf_op | source)
XLA Modules:
  0.0 425.6 jit_solution(11922655918192209739)
XLA Ops:
  7.2 0.0 copy-start
  7.2 0.0 copy-start.2
  7.2 0.0 all-gather.2.cloned.1.call-start
  7.2 0.7 all-gather.2.cloned.1.call-update
  7.9 0.0 copy-done.2
  7.9 0.1 fusion.13
  8.0 0.2 reduce_window_sum.11
  8.2 0.2 select_reduce_fusion
  8.4 7.0 %scatter_custom_fusion = bf16[256,8192]{1,0:T(8,128)(2,1)} fusion(s32[128]{0:T(128)S(1)} %fusion.14, bf16[128,8192]{1,0:T(8,128)(2,1)} %param.6, bf16[]{:T(256)} %constant.5.clone.1), kind=kCustom, calls=%fused_computation.4 | custom fusion | bytes 4194816 | tf_op jit(solution)/shard_map/scatter | solution.py:36
  15.4 7.4 %all-to-all-start = ((bf16[16,16,8192]{2,1,0:T(8,128)(2,1)}), bf16[16,16,8192]{2,1,0:T(8,128)(2,1)}, u32[]{:S(2)}, u32[]{:S(2)}) async-start(bf16[16,16,8192]{2,1,0:T(8,128)(2,1)} %bitcast.34), calls=%async_computation | async-start | bytes 8388608 | tf_op jit(solution)/shard_map/all_to_all | solution.py:44
  22.8 0.0 copy-start.1
  22.8 2.4 scatter_custom_fusion.1
  25.3 138.0 %all-to-all-done = bf16[16,16,8192]{2,1,0:T(8,128)(2,1)} async-done(((bf16[16,16,8192]{2,1,0:T(8,128)(2,1)}), bf16[16,16,8192]{2,1,0:T(8,128)(2,1)}, u32[]{:S(2)}, u32[]{:S(2)}) %all-to-all-start) | async-done | bytes 4194336 | tf_op jit(solution)/shard_map/all_to_all | solution.py:44
  163.3 67.7 %all-to-all-start.2 = ((bf16[16,16,1024]{2,1,0:T(8,128)(2,1)}), bf16[16,16,1024]{2,1,0:T(8,128)(2,1)S(1)}, u32[]{:S(2)}, u32[]{:S(2)}) async-start(bf16[16,16,1024]{2,1,0:T(8,128)(2,1)} %bitcast.9), calls=%async_computation.2 | async-start | bytes 1048576 | tf_op jit(solution)/shard_map/all_to_all | solution.py:51
  231.0 0.0 copy-done
  231.0 3.7 convolution_convert_fusion
  234.7 0.0 copy-done.1
  234.7 1.1 fusion.2
  235.8 19.2 %all-to-all-done.2 = bf16[16,16,1024]{2,1,0:T(8,128)(2,1)S(1)} async-done(((bf16[16,16,1024]{2,1,0:T(8,128)(2,1)}), bf16[16,16,1024]{2,1,0:T(8,128)(2,1)S(1)}, u32[]{:S(2)}, u32[]{:S(2)}) %all-to-all-start.2) | async-done | bytes 524320 | tf_op jit(solution)/shard_map/all_to_all | solution.py:51
  255.0 6.2 %all-to-all-start.1 = ((bf16[16,16,1024]{2,1,0:T(8,128)(2,1)}), bf16[16,16,1024]{2,1,0:T(8,128)(2,1)S(1)}, u32[]{:S(2)}, u32[]{:S(2)}) async-start(bf16[16,16,1024]{2,1,0:T(8,128)(2,1)} %bitcast.7), calls=%async_computation.1 | async-start | bytes 1048576 | tf_op jit(solution)/shard_map/all_to_all | solution.py:81
  261.2 0.9 fusion.4
  262.1 4.9 %convolution_bitcast_fusion = f32[1,8192,64]{1,2,0:T(8,128)} fusion(bf16[256,8192]{1,0:T(8,128)(2,1)} %bitcast.4, bf16[256,1024]{1,0:T(8,128)(2,1)S(1)} %bitcast.37, bf16[1,64,1024]{2,1,0:T(8,128)(2,1)S(1)} %copy-done.1), kind=kOutput, calls=%fused_computation.3 | convolution fusion | flops 302022656 | bytes 6946816 | tf_op jit(solution)/shard_map/dot_general | solution.py:78
  267.0 19.0 %all-to-all-done.1 = bf16[16,16,1024]{2,1,0:T(8,128)(2,1)S(1)} async-done(((bf16[16,16,1024]{2,1,0:T(8,128)(2,1)}), bf16[16,16,1024]{2,1,0:T(8,128)(2,1)S(1)}, u32[]{:S(2)}, u32[]{:S(2)}) %all-to-all-start.1) | async-done | bytes 524320 | tf_op jit(solution)/shard_map/all_to_all | solution.py:81
  285.9 0.9 gather_fusion
  286.8 122.5 %all-gather.2.cloned.1.call-done = bf16[8192,1024]{1,0:T(8,128)(2,1)} async-done(((bf16[2048,1024]{1,0:T(8,128)(2,1)}), bf16[8192,1024]{1,0:T(8,128)(2,1)}) %all-gather.2.cloned.1.call-update) | async-done | bytes 16777232 | tf_op jit(solution)/shard_map/all_gather | solution.py:25
  409.3 9.4 %fusion.3 = bf16[128,1024]{1,0:T(8,128)(2,1)} fusion(bf16[128,8192]{1,0:T(8,128)(2,1)} %param.6, bf16[8192,1024]{1,0:T(8,128)(2,1)} %all-gather.2.cloned.1.call-done, bf16[128,1024]{1,0:T(8,128)(2,1)S(1)} %gather_fusion), kind=kOutput, calls=%fused_computation.9 | convolution fusion | flops 2147876864 | bytes 19398656 | tf_op jit(solution)/shard_map/dot_general | solution.py:23
  (2 shorter events, 0.0 us)
Async XLA Ops:
  7.2 223.8 %copy-start = (bf16[1,8192,64]{1,2,0:T(8,128)(2,1)S(1)}, bf16[1,8192,64]{1,2,0:T(8,128)(2,1)}, u32[]{:S(2)}) copy-start(bf16[1,8192,64]{1,2,0:T(8,128)(2,1)} %param.9) | copy-start | bytes 3145732
  7.2 0.7 copy-start.2
  7.2 402.1 %all-gather.2.cloned.1.call-start = ((), (), s32[]{:S(2)}) async-start(), calls=%async_computation.3 | async-start | bytes 20971520 | tf_op jit(solution)/shard_map/all_gather | solution.py:25
  15.4 147.8 %all-to-all-start = ((bf16[16,16,8192]{2,1,0:T(8,128)(2,1)}), bf16[16,16,8192]{2,1,0:T(8,128)(2,1)}, u32[]{:S(2)}, u32[]{:S(2)}) async-start(bf16[16,16,8192]{2,1,0:T(8,128)(2,1)} %bitcast.34), calls=%async_computation | async-start | bytes 8388608 | tf_op jit(solution)/shard_map/all_to_all | solution.py:44
  22.8 211.9 %copy-start.1 = (bf16[1,64,1024]{2,1,0:T(8,128)(2,1)S(1)}, bf16[1,64,1024]{2,1,0:T(8,128)(2,1)}, u32[]{:S(2)}) copy-start(bf16[1,64,1024]{2,1,0:T(8,128)(2,1)} %param.10) | copy-start | bytes 393220
  163.3 91.8 %all-to-all-start.2 = ((bf16[16,16,1024]{2,1,0:T(8,128)(2,1)}), bf16[16,16,1024]{2,1,0:T(8,128)(2,1)S(1)}, u32[]{:S(2)}, u32[]{:S(2)}) async-start(bf16[16,16,1024]{2,1,0:T(8,128)(2,1)} %bitcast.9), calls=%async_computation.2 | async-start | bytes 1048576 | tf_op jit(solution)/shard_map/all_to_all | solution.py:51
  255.0 30.9 %all-to-all-start.1 = ((bf16[16,16,1024]{2,1,0:T(8,128)(2,1)}), bf16[16,16,1024]{2,1,0:T(8,128)(2,1)S(1)}, u32[]{:S(2)}, u32[]{:S(2)}) async-start(bf16[16,16,1024]{2,1,0:T(8,128)(2,1)} %bitcast.7), calls=%async_computation.1 | async-start | bytes 1048576 | tf_op jit(solution)/shard_map/all_to_all | solution.py:81
Sparse Core Ops, SparseCore 0:
  9.6 399.6 all-gather.1
where the time goes:
time: 426 us
  waiting for transfers between devices  299 us (70%)
  starting transfers between devices  81.3 us (19%)
  matrix products  20 us (5%)
  between operations  14.1 us (3%)
  local copies, waits for them, and re-layouts  10.4 us (2%)
    all_to_all x1, waiting for transfers between devices, per_device(): lax.all_to_all(send_x.reshape(owner_devices, slot_positions, width), ('fs...  138 us
    all_gather x1, waiting for transfers between devices, per_device(): lax.all_gather(frozen_key_weight, 'fsdp', axis=0, tiled=True)  122 us
    all_to_all x1, starting transfers between devices, per_device(): lax.all_to_all(send_dy.reshape(owner_devices, slot_positions, layer_outpu...  67.7 us
    all_to_all x1, waiting for transfers between devices, per_device(): lax.all_to_all(send_dy.reshape(owner_devices, slot_positions, layer_outpu...  19.2 us
    all_to_all x1, waiting for transfers between devices, per_device(): lax.all_to_all(adapter_term.reshape(owner_devices, slot_positions, layer_...  19 us
    dot_general x1, matrix products, per_device(): jnp.dot(rollout, lax.all_gather(frozen_key_weight, 'fsdp', axis=0, tiled=...  9.45 us
  transfers between devices with their start and end apart: 4, of which 4 were waited for; matrix products, arithmetic and copies ran while one was open for 5% of the time, Pallas kernels for 0%

commit v1 on v0

v1 whole, which is shorter than its diff:
```python
import jax
import jax.numpy as jnp
from jax import lax
from jax.sharding import PartitionSpec as P

adapter_scale = 0.5
chunks = 2
bf16, f32 = jnp.bfloat16, jnp.float32


def swap(a, axis, bits):
    n = lax.axis_size(axis)
    return lax.ppermute(a, axis, [(i, i ^ bits) for i in range(n)])


def gather(a, axis):
    held = a[None]
    bit = lax.axis_size(axis) // 2
    while bit:
        got = swap(held, axis, bit)
        held = jnp.stack([held, got], 1).reshape((-1,) + a.shape)
        bit //= 2
    return held


def exchange(pieces, axis):
    return [p if m == 0 else swap(p, axis, m) for m, p in enumerate(pieces)]


def scatter(even, odd, axis):
    bit = 1
    while True:
        even = even + swap(odd, axis, bit).astype(f32)
        bit *= 2
        if bit == lax.axis_size(axis):
            return even[0]
        pairs = even.reshape((even.shape[0] // 2, 2) + even.shape[1:])
        even, odd = pairs[:, 0], pairs[:, 1].astype(bf16)


def scatter_all(a, axis):
    pairs = a.reshape((a.shape[0] // 2, 2) + a.shape[1:])
    return scatter(pairs[:, 0], pairs[:, 1].astype(bf16), axis)


def cut(a, size, start):
    n_f = lax.axis_size("fsdp")
    depth = a.shape[1] // n_f
    f = lax.axis_index("fsdp")
    return [
        lax.dynamic_slice_in_dim(a, (f ^ n) * depth + start, size, 1) for n in range(n_f)
    ]


def dot(a, b, da, db):
    return lax.dot_general(a, b, (((da,), (db,)), ((), ())), preferred_element_type=f32)


def pick(wide, row_ids, column_ids):
    wide = wide.reshape(wide.shape[0], column_ids.shape[0], -1)
    mask = row_ids[:, None] == column_ids[None, :]
    return jnp.sum(jnp.where(mask[:, :, None], wide, 0.0), 1)


def spread(narrow, row_ids, column_ids):
    mask = row_ids[:, None] == column_ids[None, :]
    wide = jnp.where(mask[:, :, None], narrow[:, None, :], jnp.zeros((), narrow.dtype))
    return wide.reshape(narrow.shape[0], -1)


def per_device(
    rollout,
    row_adapter_index,
    frozen_key_weight,
    adapter_down_weight,
    adapter_up_weight,
    output_gradient,
):
    count, width = rollout.shape
    n_f = lax.axis_size("fsdp")
    n_r = lax.axis_size("rows")
    f = lax.axis_index("fsdp")
    r = lax.axis_index("rows")
    depth = width // n_f
    part = depth // chunks
    rank = adapter_down_weight.shape[2]
    outputs = frozen_key_weight.shape[1]
    owners = n_r * n_f

    ids = row_adapter_index[:, 0]
    down_t = jnp.swapaxes(adapter_down_weight[0], 0, 1)
    up = adapter_up_weight[0]

    ms = jnp.arange(n_r, dtype=jnp.int32)
    ns = jnp.arange(n_f, dtype=jnp.int32)
    adapters = (f ^ ns)[None, :] * n_r + (r ^ ms)[:, None]
    all_ids = adapters.reshape(-1)
    even_ids = adapters[0::2].reshape(-1)
    odd_ids = adapters[1::2].reshape(-1)

    up_own = gather(up, "fsdp")
    down_pieces = exchange(cut(down_t, depth, 0), "fsdp")
    down_own = jnp.stack(down_pieces)
    up_all = gather(up_own, "rows").reshape(owners * rank, outputs)
    down_all = gather(down_own, "rows").reshape(owners * rank, depth)

    back = (adapter_scale * pick(dot(output_gradient, up_all, 1, 1), ids, all_ids)).astype(bf16)
    packed = jnp.concatenate(
        [back, jnp.broadcast_to(ids[:, None].astype(bf16), (count, rank))], 1
    )
    packed = jnp.concatenate(exchange([packed] * n_f, "fsdp"), 0)
    back_rows = packed[:, :rank]
    row_ids = packed[:, rank].astype(jnp.int32)
    back_even = spread(back_rows, row_ids, even_ids)
    back_odd = spread(back_rows, row_ids, odd_ids)

    group = owners
    while group * rank * row_ids.shape[0] > 1 << 21 and group % 2 == 0:
        group //= 2

    def hidden_of(x_part, down_part):
        if group == owners:
            return pick(dot(x_part, down_part, 1, 1), row_ids, all_ids)

        def one(g, total):
            down = lax.dynamic_slice_in_dim(down_part, g * group * rank, group * rank, 0)
            names = lax.dynamic_slice_in_dim(all_ids, g * group, group, 0)
            return total + pick(dot(x_part, down, 1, 1), row_ids, names)

        return lax.fori_loop(
            0, owners // group, one, jnp.zeros((row_ids.shape[0], rank), f32)
        )

    base = 0.0
    hidden_part = 0.0
    grad_pieces = []
    for c in range(chunks):
        x_pieces = exchange(cut(rollout, part, c * part), "fsdp")
        x_part = jnp.concatenate(x_pieces, 0)
        odd = dot(back_odd, x_part, 0, 0).astype(bf16).reshape(n_r // 2, n_f * rank, part)
        even = dot(back_even, x_part, 0, 0).reshape(n_r // 2, n_f * rank, part)
        grad_pieces.append(scatter(even, odd, "rows"))
        span = slice(c * part, (c + 1) * part)
        base = base + dot(x_part, frozen_key_weight[span], 1, 0)
        hidden_part = hidden_part + hidden_of(x_part, down_all[:, span])

    hidden = exchange(list(hidden_part.reshape(n_f, count, rank)), "fsdp")
    hidden = sum(hidden[1:], hidden[0]).astype(bf16)
    lora = (adapter_scale * dot(spread(hidden, ids, all_ids), up_all, 1, 0)).astype(bf16)
    total = scatter_all(base.reshape(n_f, count, outputs), "fsdp")
    mixed = (total + lora.astype(f32)).astype(bf16)

    odd = adapter_scale * dot(spread(hidden, ids, odd_ids), output_gradient, 0, 0)
    even = adapter_scale * dot(spread(hidden, ids, even_ids), output_gradient, 0, 0)
    up_grad = scatter(
        even.reshape(n_r // 2, n_f * rank, outputs),
        odd.astype(bf16).reshape(n_r // 2, n_f * rank, outputs),
        "rows",
    )
    up_grad = scatter_all(up_grad.reshape(n_f, rank, outputs), "fsdp")

    grad_down = jnp.zeros((rank, width), f32)
    for c in range(chunks):
        piece = grad_pieces[c].reshape(n_f, rank, part)
        got = exchange([piece[0]] + [piece[n].astype(bf16) for n in range(1, n_f)], "fsdp")
        for n in range(n_f):
            at = (f ^ n) * depth + c * part
            grad_down = lax.dynamic_update_slice_in_dim(grad_down, got[n].astype(f32), at, 1)
    return (mixed, jnp.swapaxes(grad_down, 0, 1)[None], up_grad[None])


def solution(mesh):
    return jax.shard_map(
        per_device,
        mesh=mesh,
        in_specs=(
            P(("grp", "fsdp", "rows"), None),
            P(("grp", "fsdp", "rows"), None),
            P("fsdp", None),
            P(("grp", "fsdp", "rows"), None, None),
            P(("grp", "fsdp", "rows"), None, None),
            P(("grp", "fsdp", "rows"), None),
        ),
        out_specs=(
            P(("grp", "fsdp", "rows"), None),
            P(("grp", "fsdp", "rows"), None, None),
            P(("grp", "fsdp", "rows"), None, None),
        ),
        check_vma=False,
    )
```

time: 426 us -> 178 us (0.42)
  waiting for transfers between devices: 299 us -> 110 us
  starting transfers between devices: 81.3 us -> 45.2 us
  between operations: 14.1 us -> 1.24 us
  matrix products: 20 us -> 10.8 us
  other arithmetic: 0.44 us -> 6.64 us
  local copies, waits for them, and re-layouts: 10.4 us -> 4.54 us
    all_to_all x3 -> x0, waiting for transfers between devices: 176 us -> none  [the longest x1 138 us: per_device(): lax.all_to_all(send_x.reshape(owner_devices, slot_positions, width), ('fs...]
    all_gather x1 -> x0, waiting for transfers between devices: 122 us -> none  [per_device(): lax.all_gather(frozen_key_weight, 'fsdp', axis=0, tiled=True)]
    ppermute x0 -> x37, waiting for transfers between devices: none -> 110 us  [swap(): return lax.ppermute(a, axis, [(i, i ^ bits) for i in range(n)])]
    all_to_all x3 -> x0, starting transfers between devices: 81.3 us -> none  [the longest x1 67.7 us: per_device(): lax.all_to_all(send_dy.reshape(owner_devices, slot_positions, layer_outpu...]
    ppermute x0 -> x37, starting transfers between devices: none -> 45.2 us  [swap(): return lax.ppermute(a, axis, [(i, i ^ bits) for i in range(n)])]
    scatter x2 -> x0, local copies, waits for them, and re-layouts: 9.47 us -> none  [the longest x1 7.02 us: per_device(): send_x = jnp.zeros((owner_devices * slot_positions, width), jnp.bfloat16)...]
    dot_general x5 -> x12, matrix products: 20 us -> 10.8 us  [dot(): lax.dot_general(a, b, (((da,), (db,)), ((), ())), preferred_element_type=...]
  transfers between devices with their start and end apart: 4 -> 37, of which waited for: 4 -> 17; matrix products, arithmetic and copies ran while one was open for 5% -> 11% of each run, Pallas kernels for 0% -> 0%
where the time goes in v1:
time: 178 us
  waiting for transfers between devices  110 us (62%)
  starting transfers between devices  45.2 us (25%)
  matrix products  10.8 us (6%)
  other arithmetic  6.64 us (4%)
  local copies, waits for them, and re-layouts  4.54 us (3%)
    ppermute x37, waiting for transfers between devices, swap(): return lax.ppermute(a, axis, [(i, i ^ bits) for i in range(n)])  110 us
    ppermute x37, starting transfers between devices, swap(): return lax.ppermute(a, axis, [(i, i ^ bits) for i in range(n)])  45.2 us
    dot_general x12, matrix products, dot(): lax.dot_general(a, b, (((da,), (db,)), ((), ())), preferred_element_type=...  10.8 us
  transfers between devices with their start and end apart: 37, of which 17 were waited for; matrix products, arithmetic and copies ran while one was open for 11% of the time, Pallas kernels for 0%

profile of v1, /device:TPU:0, one launch (start us, length us, event | category | flops | bytes accessed | tf_op | source)
XLA Modules:
  0.0 178.0 jit_solution(13608036164106399020)
XLA Ops:
  0.7 2.3 %dynamic-slice_bitcast_fusion.3 = (bf16[1,64,2048]{2,1,0:T(8,128)(2,1)S(1)}, bf16[64,2048]{1,0:T(8,128)(2,1)}, bf16[64,2048]{1,0:T(8,128)(2,1)}, bf16[64,2048]{1,0:T(8,128)(2,1)}) fusion(bf16[1,8192,64]{1,2,0:T(8,128)(2,1)} %param.9, s32[]{:T(128)S(6)} %select_n.91, s32[]{:T(128)S(6)} %select_n.92, s32[]{:T(128)S(6)} %select_n.94, s32[]{:T(128)S(6)} %select_n.93), kind=kLoop, calls=%fused_computation.84 | loop fusion | bytes 2097168 | tf_op jit(solution)/shard_map/stack | solution.py:103
  2.9 3.0 %collective-permute-start.15 = (bf16[64,2048]{1,0:T(8,128)(2,1)}, bf16[64,2048]{1,0:T(8,128)(2,1)S(1)}, u32[]{:S(2)}, u32[]{:S(2)}) collective-permute-start(bf16[64,2048]{1,0:T(8,128)(2,1)} %get-tuple-element.24), channel_id=1, source_target_pairs={{0,4},{4,0},{8,12},{12,8},{1,5},{5,1},{9,13},{13,9},{2,6},{6,2},{1... | collective-permute-start | bytes 786440 | tf_op jit(solution)/shard_map/ppermute | solution.py:13
  6.0 2.6 %collective-permute-start.16 = (bf16[64,2048]{1,0:T(8,128)(2,1)}, bf16[64,2048]{1,0:T(8,128)(2,1)}, u32[]{:S(2)}, u32[]{:S(2)}) collective-permute-start(bf16[64,2048]{1,0:T(8,128)(2,1)} %get-tuple-element.26), channel_id=1, source_target_pairs={{0,8},{4,12},{8,0},{12,4},{1,9},{5,13},{9,1},{13,5},{2,10},{6,14},... | collective-permute-start | bytes 786440 | tf_op jit(solution)/shard_map/ppermute | solution.py:13
  8.6 1.9 %collective-permute-start.8 = (bf16[1,64,1024]{2,1,0:T(8,128)(2,1)}, bf16[1,64,1024]{2,1,0:T(8,128)(2,1)}, u32[]{:S(2)}, u32[]{:S(2)}) collective-permute-start(bf16[1,64,1024]{2,1,0:T(8,128)(2,1)} %param.10), channel_id=1, source_target_pairs={{0,8},{4,12},{8,0},{12,4},{1,9},{5,13},{9,1},{13,5},{2,10},{6,14},... | collective-permute-start | bytes 393224 | tf_op jit(solution)/shard_map/ppermute | solution.py:13
  10.5 1.2 constant_dynamic-slice_fusion.7
  11.6 2.5 %collective-permute-start = (bf16[128,1024]{1,0:T(8,128)(2,1)}, bf16[128,1024]{1,0:T(8,128)(2,1)S(1)}, u32[]{:S(2)}, u32[]{:S(2)}) collective-permute-start(bf16[128,1024]{1,0:T(8,128)(2,1)} %get-tuple-element.16), channel_id=1, source_target_pairs={{0,4},{4,0},{8,12},{12,8},{1,5},{5,1},{9,13},{13,9},{2,6},{6,2},{1... | collective-permute-start | bytes 786440 | tf_op jit(solution)/shard_map/ppermute | solution.py:13
  14.1 23.4 %collective-permute-done.8 = bf16[1,64,1024]{2,1,0:T(8,128)(2,1)} collective-permute-done((bf16[1,64,1024]{2,1,0:T(8,128)(2,1)}, bf16[1,64,1024]{2,1,0:T(8,128)(2,1)}, u32[]{:S(2)}, u32[]{:S(2)}) %collective-permute-start.8) | collective-permute-done | bytes 131104 | tf_op jit(solution)/shard_map/ppermute | solution.py:13
  37.5 0.9 fusion.42
  38.6 6.5 %collective-permute-done.9 = bf16[2,64,1024]{2,1,0:T(8,128)(2,1)S(1)} collective-permute-done((bf16[2,64,1024]{2,1,0:T(8,128)(2,1)S(1)}, bf16[2,64,1024]{2,1,0:T(8,128)(2,1)S(1)}, u32[]{:S(2)}, u32[]{:S(2)}) %collective-permute-start.9) | collective-permute-done | bytes 262176 | tf_op jit(solution)/shard_map/ppermute | solution.py:13
  45.2 1.6 collective-permute-start.10
  47.1 0.3 collective-permute-start.3
  47.4 2.8 %collective-permute-start.4 = (bf16[128,1024]{1,0:T(8,128)(2,1)}, bf16[128,1024]{1,0:T(8,128)(2,1)S(1)}, u32[]{:S(2)}, u32[]{:S(2)}) collective-permute-start(bf16[128,1024]{1,0:T(8,128)(2,1)} %get-tuple-element.18), channel_id=1, source_target_pairs={{0,8},{4,12},{8,0},{12,4},{1,9},{5,13},{9,1},{13,5},{2,10},{6,14},... | collective-permute-start | bytes 786440 | tf_op jit(solution)/shard_map/ppermute | solution.py:13
  50.2 1.3 collective-permute-start.5
  51.5 1.3 fusion.40
  52.9 3.6 %collective-permute-done.10 = bf16[1,4,64,1024]{3,2,1,0:T(8,128)(2,1)S(1)} collective-permute-done((bf16[1,4,64,1024]{3,2,1,0:T(8,128)(2,1)S(1)}, bf16[1,4,64,1024]{3,2,1,0:T(8,128)(2,1)S(1)}, u32[]{:S(2)}, u32[]{:S(2)}) %collective-permute-start.10) | collective-permute-done | bytes 524320 | tf_op jit(solution)/shard_map/ppermute | solution.py:13
  56.5 1.6 collective-permute-start.1
  58.3 2.6 %collective-permute-start.2 = (bf16[128,1024]{1,0:T(8,128)(2,1)S(1)}, bf16[128,1024]{1,0:T(8,128)(2,1)S(1)}, u32[]{:S(2)}, u32[]{:S(2)}) collective-permute-start(bf16[128,1024]{1,0:T(8,128)(2,1)S(1)} %copy-done.3), channel_id=1, source_target_pairs={{0,12},{4,8},{8,4},{12,0},{1,13},{5,9},{9,5},{13,1},{2,14},{6,10},... | collective-permute-start | bytes 786440 | tf_op jit(solution)/shard_map/ppermute | solution.py:13
  60.9 18.4 %collective-permute-done.4 = bf16[128,1024]{1,0:T(8,128)(2,1)S(1)} collective-permute-done((bf16[128,1024]{1,0:T(8,128)(2,1)}, bf16[128,1024]{1,0:T(8,128)(2,1)S(1)}, u32[]{:S(2)}, u32[]{:S(2)}) %collective-permute-start.4) | collective-permute-done | bytes 262176 | tf_op jit(solution)/shard_map/ppermute | solution.py:13
  79.3 0.5 collective-permute-start.18
  79.9 1.3 fusion.4
  81.1 9.4 %collective-permute-done.1 = bf16[128,1024]{1,0:T(8,128)(2,1)S(1)} collective-permute-done((bf16[128,1024]{1,0:T(8,128)(2,1)S(1)}, bf16[128,1024]{1,0:T(8,128)(2,1)S(1)}, u32[]{:S(2)}, u32[]{:S(2)}) %collective-permute-start.1) | collective-permute-done | bytes 262176 | tf_op jit(solution)/shard_map/ppermute | solution.py:13
  90.5 1.3 fusion.8
  91.9 3.4 %collective-permute-start.6 = (bf16[2,128,1024]{2,1,0:T(8,128)(2,1)S(1)}, bf16[2,128,1024]{2,1,0:T(8,128)(2,1)S(1)}, u32[]{:S(2)}, u32[]{:S(2)}) collective-permute-start(bf16[2,128,1024]{2,1,0:T(8,128)(2,1)S(1)} %fusion.27), channel_id=1, source_target_pairs={{0,4},{4,0},{8,12},{12,8},{1,5},{5,1},{9,13},{13,9},{2,6},{6,2},{1... | collective-permute-start | bytes 1572872 | tf_op jit(solution)/shard_map/ppermute | solution.py:13
  95.7 0.7 fusion.52
  96.6 3.0 %collective-permute-start.13 = (bf16[128,128]{0,1:T(8,128)(2,1)S(1)}, bf16[128,128]{0,1:T(8,128)(2,1)S(1)}, u32[]{:S(2)}, u32[]{:S(2)}) collective-permute-start(bf16[128,128]{0,1:T(8,128)(2,1)S(1)} %pad_maximum_fusion.13), channel_id=1, source_target_pairs={{0,8},{4,12},{8,0},{12,4},{1,9},{5,13},{9,1},{13,5},{2,10},{6,14},... | collective-permute-start | bytes 98312 | tf_op jit(solution)/shard_map/ppermute | solution.py:13
  99.6 1.3 collective-permute-start.14
  101.0 0.3 fusion.12
  101.3 5.1 %collective-permute-done.12 = bf16[128,128]{0,1:T(8,128)(2,1)S(1)} collective-permute-done((bf16[128,128]{0,1:T(8,128)(2,1)S(1)}, bf16[128,128]{0,1:T(8,128)(2,1)S(1)}, u32[]{:S(2)}, u32[]{:S(2)}) %collective-permute-start.12) | collective-permute-done | bytes 32800 | tf_op jit(solution)/shard_map/ppermute | solution.py:13
  106.4 3.1 %collective-permute-done.14 = bf16[128,128]{0,1:T(8,128)(2,1)S(1)} collective-permute-done((bf16[128,128]{0,1:T(8,128)(2,1)S(1)}, bf16[128,128]{0,1:T(8,128)(2,1)S(1)}, u32[]{:S(2)}, u32[]{:S(2)}) %collective-permute-start.14) | collective-permute-done | bytes 32800 | tf_op jit(solution)/shard_map/ppermute | solution.py:13
  109.7 0.7 convolution_convert_fusion
  110.6 0.7 convolution_convert_fusion.1
  111.3 0.6 collective-permute-start.23
  112.3 0.9 collective-permute-done.28
  113.2 0.8 add_bitcast_fusion.1
  114.0 0.6 collective-permute-start.29
  114.7 0.7 add_bitcast_fusion.2
  115.4 0.4 pad_maximum_fusion
  115.8 1.3 fusion.2
  117.1 1.3 fusion
  118.4 0.5 select_reduce_fusion
  119.0 0.4 collective-permute-start.20
  119.4 1.8 %collective-permute-start.21 = (f32[128,64]{0,1:T(8,128)S(1)}, f32[128,64]{0,1:T(8,128)S(1)}, u32[]{:S(2)}, u32[]{:S(2)}) collective-permute-start(f32[128,64]{0,1:T(8,128)S(1)} %get-tuple-element.37), channel_id=1, source_target_pairs={{0,8},{4,12},{8,0},{12,4},{1,9},{5,13},{9,1},{13,5},{2,10},{6,14},... | collective-permute-start | bytes 98312 | tf_op jit(solution)/shard_map/ppermute | solution.py:13
  121.2 2.2 %collective-permute-start.22 = (f32[128,64]{0,1:T(8,128)S(1)}, f32[128,64]{0,1:T(8,128)S(1)}, u32[]{:S(2)}, u32[]{:S(2)}) collective-permute-start(f32[128,64]{0,1:T(8,128)S(1)} %get-tuple-element.36), channel_id=1, source_target_pairs={{0,12},{4,8},{8,4},{12,0},{1,13},{5,9},{9,5},{13,1},{2,14},{6,10},... | collective-permute-start | bytes 98312 | tf_op jit(solution)/shard_map/ppermute | solution.py:13
  123.5 1.8 %collective-permute-done.20 = f32[128,64]{0,1:T(8,128)S(1)} collective-permute-done((f32[128,64]{0,1:T(8,128)S(1)}, f32[128,64]{0,1:T(8,128)S(1)}, u32[]{:S(2)}, u32[]{:S(2)}) %collective-permute-start.20) | collective-permute-done | bytes 32800 | tf_op jit(solution)/shard_map/ppermute | solution.py:13
  125.3 1.6 collective-permute-start.24
  126.9 1.9 %collective-permute-done.21 = f32[128,64]{0,1:T(8,128)S(1)} collective-permute-done((f32[128,64]{0,1:T(8,128)S(1)}, f32[128,64]{0,1:T(8,128)S(1)}, u32[]{:S(2)}, u32[]{:S(2)}) %collective-permute-start.21) | collective-permute-done | bytes 32800 | tf_op jit(solution)/shard_map/ppermute | solution.py:13
  128.9 0.4 multiply_convert_fusion
  129.4 0.4 convolution_multiply_fusion
  129.8 1.2 fusion.33
  131.0 8.2 %collective-permute-done.24 = bf16[1,256,1024]{2,1,0:T(8,128)(2,1)S(1)} collective-permute-done((bf16[1,256,1024]{2,1,0:T(8,128)(2,1)S(1)}, bf16[1,256,1024]{2,1,0:T(8,128)(2,1)S(1)}, u32[]{:S(2)}, u32[]{:S(2)}) %collective-permute-start.24) | collective-permute-done | bytes 524320 | tf_op jit(solution)/shard_map/ppermute | solution.py:13
  139.5 0.3 collective-permute-start.25
  139.8 1.9 %collective-permute-start.26 = (bf16[64,1024]{1,0:T(8,128)(2,1)S(1)}, bf16[64,1024]{1,0:T(8,128)(2,1)S(1)}, u32[]{:S(2)}, u32[]{:S(2)}) collective-permute-start(bf16[64,1024]{1,0:T(8,128)(2,1)S(1)} %get-tuple-element.31), channel_id=1, source_target_pairs={{0,8},{4,12},{8,0},{12,4},{1,9},{5,13},{9,1},{13,5},{2,10},{6,14},... | collective-permute-start | bytes 393224 | tf_op jit(solution)/shard_map/ppermute | solution.py:13
  141.8 2.2 %collective-permute-start.27 = (bf16[64,1024]{1,0:T(8,128)(2,1)S(1)}, bf16[64,1024]{1,0:T(8,128)(2,1)S(1)}, u32[]{:S(2)}, u32[]{:S(2)}) collective-permute-start(bf16[64,1024]{1,0:T(8,128)(2,1)S(1)} %get-tuple-element.30), channel_id=1, source_target_pairs={{0,12},{4,8},{8,4},{12,0},{1,13},{5,9},{9,5},{13,1},{2,14},{6,10},... | collective-permute-start | bytes 393224 | tf_op jit(solution)/shard_map/ppermute | solution.py:13
  144.5 3.3 %collective-permute-done.25 = bf16[64,1024]{1,0:T(8,128)(2,1)S(1)} collective-permute-done((bf16[64,1024]{1,0:T(8,128)(2,1)S(1)}, bf16[64,1024]{1,0:T(8,128)(2,1)S(1)}, u32[]{:S(2)}, u32[]{:S(2)}) %collective-permute-start.25) | collective-permute-done | bytes 131104 | tf_op jit(solution)/shard_map/ppermute | solution.py:13
  147.9 1.5 collective-permute-start.32
  149.3 0.4 add_bitcast_fusion
  149.9 3.1 %collective-permute-done.26 = bf16[64,1024]{1,0:T(8,128)(2,1)S(1)} collective-permute-done((bf16[64,1024]{1,0:T(8,128)(2,1)S(1)}, bf16[64,1024]{1,0:T(8,128)(2,1)S(1)}, u32[]{:S(2)}, u32[]{:S(2)}) %collective-permute-start.26) | collective-permute-done | bytes 131104 | tf_op jit(solution)/shard_map/ppermute | solution.py:13
  152.9 1.2 collective-permute-start.34
  154.3 7.9 %collective-permute-done.34 = bf16[1,256,1024]{2,1,0:T(8,128)(2,1)S(1)} collective-permute-done((bf16[1,256,1024]{2,1,0:T(8,128)(2,1)S(1)}, bf16[1,256,1024]{2,1,0:T(8,128)(2,1)S(1)}, u32[]{:S(2)}, u32[]{:S(2)}) %collective-permute-start.34) | collective-permute-done | bytes 524320 | tf_op jit(solution)/shard_map/ppermute | solution.py:13
  162.5 0.9 collective-permute-done.31
  163.4 6.4 %collective-permute-done.35 = bf16[2,64,1024]{2,1,0:T(8,128)(2,1)S(1)} collective-permute-done((bf16[2,64,1024]{2,1,0:T(8,128)(2,1)S(1)}, bf16[2,64,1024]{2,1,0:T(8,128)(2,1)S(1)}, u32[]{:S(2)}, u32[]{:S(2)}) %collective-permute-start.35) | collective-permute-done | bytes 262176 | tf_op jit(solution)/shard_map/ppermute | solution.py:13
  169.9 1.7 collective-permute-start.36
  171.7 5.6 %collective-permute-done.36 = bf16[1,64,1024]{2,1,0:T(8,128)(2,1)S(1)} collective-permute-done((bf16[1,64,1024]{2,1,0:T(8,128)(2,1)S(1)}, bf16[1,64,1024]{2,1,0:T(8,128)(2,1)S(1)}, u32[]{:S(2)}, u32[]{:S(2)}) %collective-permute-start.36) | collective-permute-done | bytes 131104 | tf_op jit(solution)/shard_map/ppermute | solution.py:13
  177.3 0.7 fusion.36
  (98 shorter events, 3.8 us)
Async XLA Ops:
  0.6 95.0 %copy-start = (bf16[128,1024]{1,0:T(8,128)(2,1)S(1)}, bf16[128,1024]{1,0:T(8,128)(2,1)}, u32[]{:S(2)}) copy-start(bf16[128,1024]{1,0:T(8,128)(2,1)} %param.11) | copy-start | bytes 786436
  0.6 9.8 %copy-start.1 = (bf16[128,8192]{1,0:T(8,128)(2,1)S(1)}, bf16[128,8192]{1,0:T(8,128)(2,1)}, u32[]{:S(2)}) copy-start(bf16[128,8192]{1,0:T(8,128)(2,1)} %param.6) | copy-start | bytes 6291460
  2.9 44.2 %collective-permute-start.15 = (bf16[64,2048]{1,0:T(8,128)(2,1)}, bf16[64,2048]{1,0:T(8,128)(2,1)S(1)}, u32[]{:S(2)}, u32[]{:S(2)}) collective-permute-start(bf16[64,2048]{1,0:T(8,128)(2,1)} %get-tuple-element.24), channel_id=1, source_target_pairs={{0,4},{4,0},{8,12},{12,8},{1,5},{5,1},{9,13},{13,9},{2,6},{6,2},{1... | collective-permute-start | bytes 786440 | tf_op jit(solution)/shard_map/ppermute | solution.py:13
  6.0 41.5 %collective-permute-start.16 = (bf16[64,2048]{1,0:T(8,128)(2,1)}, bf16[64,2048]{1,0:T(8,128)(2,1)}, u32[]{:S(2)}, u32[]{:S(2)}) collective-permute-start(bf16[64,2048]{1,0:T(8,128)(2,1)} %get-tuple-element.26), channel_id=1, source_target_pairs={{0,8},{4,12},{8,0},{12,4},{1,9},{5,13},{9,1},{13,5},{2,10},{6,14},... | collective-permute-start | bytes 786440 | tf_op jit(solution)/shard_map/ppermute | solution.py:13
  8.6 41.6 %collective-permute-start.17 = (bf16[64,2048]{1,0:T(8,128)(2,1)}, bf16[64,2048]{1,0:T(8,128)(2,1)}, u32[]{:S(2)}, u32[]{:S(2)}) collective-permute-start(bf16[64,2048]{1,0:T(8,128)(2,1)} %get-tuple-element.25), channel_id=1, source_target_pairs={{0,12},{4,8},{8,4},{12,0},{1,13},{5,9},{9,5},{13,1},{2,14},{6,10},... | collective-permute-start | bytes 786440 | tf_op jit(solution)/shard_map/ppermute | solution.py:13
  8.6 28.9 %collective-permute-start.8 = (bf16[1,64,1024]{2,1,0:T(8,128)(2,1)}, bf16[1,64,1024]{2,1,0:T(8,128)(2,1)}, u32[]{:S(2)}, u32[]{:S(2)}) collective-permute-start(bf16[1,64,1024]{2,1,0:T(8,128)(2,1)} %param.10), channel_id=1, source_target_pairs={{0,8},{4,12},{8,0},{12,4},{1,9},{5,13},{9,1},{13,5},{2,10},{6,14},... | collective-permute-start | bytes 393224 | tf_op jit(solution)/shard_map/ppermute | solution.py:13
  10.5 27.0 %copy-start.5 = (bf16[1,64,1024]{2,1,0:T(8,128)(2,1)S(1)}, bf16[1,64,1024]{2,1,0:T(8,128)(2,1)}, u32[]{:S(2)}) copy-start(bf16[1,64,1024]{2,1,0:T(8,128)(2,1)} %param.10) | copy-start | bytes 393220
  10.5 36.3 %copy-start.6 = (s32[128,1]{0,1:T(1,128)S(1)}, s32[128,1]{0,1:T(1,128)}, u32[]{:S(2)}) copy-start(s32[128,1]{0,1:T(1,128)} %param.7) | copy-start | bytes 1540
  11.6 69.5 %collective-permute-start = (bf16[128,1024]{1,0:T(8,128)(2,1)}, bf16[128,1024]{1,0:T(8,128)(2,1)S(1)}, u32[]{:S(2)}, u32[]{:S(2)}) collective-permute-start(bf16[128,1024]{1,0:T(8,128)(2,1)} %get-tuple-element.16), channel_id=1, source_target_pairs={{0,4},{4,0},{8,12},{12,8},{1,5},{5,1},{9,13},{13,9},{2,6},{6,2},{1... | collective-permute-start | bytes 786440 | tf_op jit(solution)/shard_map/ppermute | solution.py:13
  38.4 6.7 %collective-permute-start.9 = (bf16[2,64,1024]{2,1,0:T(8,128)(2,1)S(1)}, bf16[2,64,1024]{2,1,0:T(8,128)(2,1)S(1)}, u32[]{:S(2)}, u32[]{:S(2)}) collective-permute-start(bf16[2,64,1024]{2,1,0:T(8,128)(2,1)S(1)} %get-tuple-element.34), channel_id=1, source_target_pairs={{0,4},{4,0},{8,12},{12,8},{1,5},{5,1},{9,13},{13,9},{2,6},{6,2},{1... | collective-permute-start | bytes 786440 | tf_op jit(solution)/shard_map/ppermute | solution.py:13
  45.1 11.4 %copy-start.4 = (bf16[128,1024]{1,0:T(8,128)(2,1)S(1)}, bf16[128,1024]{1,0:T(8,128)(2,1)}, u32[]{:S(2)}) copy-start(bf16[128,1024]{1,0:T(8,128)(2,1)} %get-tuple-element.15) | copy-start | bytes 786436
  45.2 11.4 %collective-permute-start.10 = (bf16[1,4,64,1024]{3,2,1,0:T(8,128)(2,1)S(1)}, bf16[1,4,64,1024]{3,2,1,0:T(8,128)(2,1)S(1)}, u32[]{:S(2)}, u32[]{:S(2)}) collective-permute-start(bf16[1,4,64,1024]{3,2,1,0:T(8,128)(2,1)S(1)} %bitcast.199), channel_id=1, source_target_pairs={{0,2},{1,3},{2,0},{3,1},{4,6},{5,7},{6,4},{7,5},{8,10},{9,11},{10,... | collective-permute-start | bytes 1572872 | tf_op jit(solution)/shard_map/ppermute | solution.py:13
  47.1 11.2 %collective-permute-start.3 = (bf16[128,1024]{1,0:T(8,128)(2,1)}, bf16[128,1024]{1,0:T(8,128)(2,1)S(1)}, u32[]{:S(2)}, u32[]{:S(2)}) collective-permute-start(bf16[128,1024]{1,0:T(8,128)(2,1)} %get-tuple-element.12), channel_id=1, source_target_pairs={{0,4},{4,0},{8,12},{12,8},{1,5},{5,1},{9,13},{13,9},{2,6},{6,2},{1... | collective-permute-start | bytes 786440 | tf_op jit(solution)/shard_map/ppermute | solution.py:13
  47.4 31.9 %collective-permute-start.4 = (bf16[128,1024]{1,0:T(8,128)(2,1)}, bf16[128,1024]{1,0:T(8,128)(2,1)S(1)}, u32[]{:S(2)}, u32[]{:S(2)}) collective-permute-start(bf16[128,1024]{1,0:T(8,128)(2,1)} %get-tuple-element.18), channel_id=1, source_target_pairs={{0,8},{4,12},{8,0},{12,4},{1,9},{5,13},{9,1},{13,5},{2,10},{6,14},... | collective-permute-start | bytes 786440 | tf_op jit(solution)/shard_map/ppermute | solution.py:13
  50.2 29.7 %collective-permute-start.5 = (bf16[128,1024]{1,0:T(8,128)(2,1)}, bf16[128,1024]{1,0:T(8,128)(2,1)S(1)}, u32[]{:S(2)}, u32[]{:S(2)}) collective-permute-start(bf16[128,1024]{1,0:T(8,128)(2,1)} %get-tuple-element.17), channel_id=1, source_target_pairs={{0,12},{4,8},{8,4},{12,0},{1,13},{5,9},{9,5},{13,1},{2,14},{6,10},... | collective-permute-start | bytes 786440 | tf_op jit(solution)/shard_map/ppermute | solution.py:13
  51.5 28.3 %copy-start.7 = (bf16[2048,1024]{1,0:T(8,128)(2,1)S(1)}, bf16[2048,1024]{1,0:T(8,128)(2,1)}, u32[]{:S(2)}) copy-start(bf16[2048,1024]{1,0:T(8,128)(2,1)} %param.8) | copy-start | bytes 12582916
  52.9 5.4 %copy-start.3 = (bf16[128,1024]{1,0:T(8,128)(2,1)S(1)}, bf16[128,1024]{1,0:T(8,128)(2,1)}, u32[]{:S(2)}) copy-start(bf16[128,1024]{1,0:T(8,128)(2,1)} %get-tuple-element.14) | copy-start | bytes 786436
  56.5 34.0 %collective-permute-start.1 = (bf16[128,1024]{1,0:T(8,128)(2,1)S(1)}, bf16[128,1024]{1,0:T(8,128)(2,1)S(1)}, u32[]{:S(2)}, u32[]{:S(2)}) collective-permute-start(bf16[128,1024]{1,0:T(8,128)(2,1)S(1)} %copy-done.4), channel_id=1, source_target_pairs={{0,8},{4,12},{8,0},{12,4},{1,9},{5,13},{9,1},{13,5},{2,10},{6,14},... | collective-permute-start | bytes 786440 | tf_op jit(solution)/shard_map/ppermute | solution.py:13
  58.3 32.2 %collective-permute-start.2 = (bf16[128,1024]{1,0:T(8,128)(2,1)S(1)}, bf16[128,1024]{1,0:T(8,128)(2,1)S(1)}, u32[]{:S(2)}, u32[]{:S(2)}) collective-permute-start(bf16[128,1024]{1,0:T(8,128)(2,1)S(1)} %copy-done.3), channel_id=1, source_target_pairs={{0,12},{4,8},{8,4},{12,0},{1,13},{5,9},{9,5},{13,1},{2,14},{6,10},... | collective-permute-start | bytes 786440 | tf_op jit(solution)/shard_map/ppermute | solution.py:13
  79.3 21.6 %collective-permute-start.18 = (bf16[1,4,64,2048]{3,2,1,0:T(8,128)(2,1)S(1)}, bf16[1,4,64,2048]{3,2,1,0:T(8,128)(2,1)S(1)}, u32[]{:S(2)}, u32[]{:S(2)}) collective-permute-start(bf16[1,4,64,2048]{3,2,1,0:T(8,128)(2,1)S(1)} %get-tuple-element.22), channel_id=1, source_target_pairs={{0,2},{1,3},{2,0},{3,1},{4,6},{5,7},{6,4},{7,5},{8,10},{9,11},{10,... | collective-permute-start | bytes 3145736 | tf_op jit(solution)/shard_map/ppermute | solution.py:13
  79.9 15.4 %collective-permute-start.11 = (bf16[2,4,64,1024]{3,2,1,0:T(8,128)(2,1)S(1)}, bf16[2,4,64,1024]{3,2,1,0:T(8,128)(2,1)S(1)}, u32[]{:S(2)}, u32[]{:S(2)}) collective-permute-start(bf16[2,4,64,1024]{3,2,1,0:T(8,128)(2,1)S(1)} %get-tuple-element.20), channel_id=1, source_target_pairs={{0,1},{1,0},{2,3},{3,2},{4,5},{5,4},{6,7},{7,6},{8,9},{9,8},{10,11... | collective-permute-start | bytes 3145736 | tf_op jit(solution)/shard_map/ppermute | solution.py:13
  91.9 20.0 %collective-permute-start.6 = (bf16[2,128,1024]{2,1,0:T(8,128)(2,1)S(1)}, bf16[2,128,1024]{2,1,0:T(8,128)(2,1)S(1)}, u32[]{:S(2)}, u32[]{:S(2)}) collective-permute-start(bf16[2,128,1024]{2,1,0:T(8,128)(2,1)S(1)} %fusion.27), channel_id=1, source_target_pairs={{0,4},{4,0},{8,12},{12,8},{1,5},{5,1},{9,13},{13,9},{2,6},{6,2},{1... | collective-permute-start | bytes 1572872 | tf_op jit(solution)/shard_map/ppermute | solution.py:13
  96.5 9.9 %collective-permute-start.12 = (bf16[128,128]{0,1:T(8,128)(2,1)S(1)}, bf16[128,128]{0,1:T(8,128)(2,1)S(1)}, u32[]{:S(2)}, u32[]{:S(2)}) collective-permute-start(bf16[128,128]{0,1:T(8,128)(2,1)S(1)} %pad_maximum_fusion.13), channel_id=1, source_target_pairs={{0,4},{4,0},{8,12},{12,8},{1,5},{5,1},{9,13},{13,9},{2,6},{6,2},{1... | collective-permute-start | bytes 98312 | tf_op jit(solution)/shard_map/ppermute | solution.py:13
  96.6 9.8 %collective-permute-start.13 = (bf16[128,128]{0,1:T(8,128)(2,1)S(1)}, bf16[128,128]{0,1:T(8,128)(2,1)S(1)}, u32[]{:S(2)}, u32[]{:S(2)}) collective-permute-start(bf16[128,128]{0,1:T(8,128)(2,1)S(1)} %pad_maximum_fusion.13), channel_id=1, source_target_pairs={{0,8},{4,12},{8,0},{12,4},{1,9},{5,13},{9,1},{13,5},{2,10},{6,14},... | collective-permute-start | bytes 98312 | tf_op jit(solution)/shard_map/ppermute | solution.py:13
  99.6 9.9 %collective-permute-start.14 = (bf16[128,128]{0,1:T(8,128)(2,1)S(1)}, bf16[128,128]{0,1:T(8,128)(2,1)S(1)}, u32[]{:S(2)}, u32[]{:S(2)}) collective-permute-start(bf16[128,128]{0,1:T(8,128)(2,1)S(1)} %pad_maximum_fusion.13), channel_id=1, source_target_pairs={{0,12},{4,8},{8,4},{12,0},{1,13},{5,9},{9,5},{13,1},{2,14},{6,10},... | collective-permute-start | bytes 98312 | tf_op jit(solution)/shard_map/ppermute | solution.py:13
  101.2 14.2 %collective-permute-start.19 = (bf16[2,4,64,2048]{3,2,1,0:T(8,128)(2,1)S(1)}, bf16[2,4,64,2048]{3,2,1,0:T(8,128)(2,1)S(1)}, u32[]{:S(2)}, u32[]{:S(2)}) collective-permute-start(bf16[2,4,64,2048]{3,2,1,0:T(8,128)(2,1)S(1)} %get-tuple-element.10), channel_id=1, source_target_pairs={{0,1},{1,0},{2,3},{3,2},{4,5},{5,4},{6,7},{7,6},{8,9},{9,8},{10,11... | collective-permute-start | bytes 6291464 | tf_op jit(solution)/shard_map/ppermute | solution.py:13
  110.4 2.7 %collective-permute-start.28 = (bf16[2,256,1024]{2,1,0:T(8,128)(2,1)S(1)}, bf16[2,256,1024]{2,1,0:T(8,128)(2,1)S(1)}, u32[]{:S(2)}, u32[]{:S(2)}) collective-permute-start(bf16[2,256,1024]{2,1,0:T(8,128)(2,1)S(1)} %bitcast.224), channel_id=1, source_target_pairs={{0,1},{1,0},{2,3},{3,2},{4,5},{5,4},{6,7},{7,6},{8,9},{9,8},{10,11... | collective-permute-start | bytes 3145736 | tf_op jit(solution)/shard_map/ppermute | solution.py:13
  111.3 3.3 %collective-permute-start.23 = (bf16[2,256,1024]{2,1,0:T(8,128)(2,1)S(1)}, bf16[2,256,1024]{2,1,0:T(8,128)(2,1)S(1)}, u32[]{:S(2)}, u32[]{:S(2)}) collective-permute-start(bf16[2,256,1024]{2,1,0:T(8,128)(2,1)S(1)} %bitcast.223), channel_id=1, source_target_pairs={{0,1},{1,0},{2,3},{3,2},{4,5},{5,4},{6,7},{7,6},{8,9},{9,8},{10,11... | collective-permute-start | bytes 3145736 | tf_op jit(solution)/shard_map/ppermute | solution.py:13
  112.1 17.7 %collective-permute-start.7 = (bf16[1,128,1024]{2,1,0:T(8,128)(2,1)S(1)}, bf16[1,128,1024]{2,1,0:T(8,128)(2,1)S(1)}, u32[]{:S(2)}, u32[]{:S(2)}) collective-permute-start(bf16[1,128,1024]{2,1,0:T(8,128)(2,1)S(1)} %fusion.34), channel_id=1, source_target_pairs={{0,8},{4,12},{8,0},{12,4},{1,9},{5,13},{9,1},{13,5},{2,10},{6,14},... | collective-permute-start | bytes 786440 | tf_op jit(solution)/shard_map/ppermute | solution.py:13
  114.0 30.0 %collective-permute-start.29 = (bf16[1,256,1024]{2,1,0:T(8,128)(2,1)S(1)}, bf16[1,256,1024]{2,1,0:T(8,128)(2,1)S(1)}, u32[]{:S(2)}, u32[]{:S(2)}) collective-permute-start(bf16[1,256,1024]{2,1,0:T(8,128)(2,1)S(1)} %fusion.25), channel_id=1, source_target_pairs={{0,2},{1,3},{2,0},{3,1},{4,6},{5,7},{6,4},{7,5},{8,10},{9,11},{10,... | collective-permute-start | bytes 1572872 | tf_op jit(solution)/shard_map/ppermute | solution.py:13
  119.0 6.4 %collective-permute-start.20 = (f32[128,64]{0,1:T(8,128)S(1)}, f32[128,64]{0,1:T(8,128)S(1)}, u32[]{:S(2)}, u32[]{:S(2)}) collective-permute-start(f32[128,64]{0,1:T(8,128)S(1)} %get-tuple-element.35), channel_id=1, source_target_pairs={{0,4},{4,0},{8,12},{12,8},{1,5},{5,1},{9,13},{13,9},{2,6},{6,2},{1... | collective-permute-start | bytes 98312 | tf_op jit(solution)/shard_map/ppermute | solution.py:13
  119.4 9.4 %collective-permute-start.21 = (f32[128,64]{0,1:T(8,128)S(1)}, f32[128,64]{0,1:T(8,128)S(1)}, u32[]{:S(2)}, u32[]{:S(2)}) collective-permute-start(f32[128,64]{0,1:T(8,128)S(1)} %get-tuple-element.37), channel_id=1, source_target_pairs={{0,8},{4,12},{8,0},{12,4},{1,9},{5,13},{9,1},{13,5},{2,10},{6,14},... | collective-permute-start | bytes 98312 | tf_op jit(solution)/shard_map/ppermute | solution.py:13
  121.2 7.6 %collective-permute-start.22 = (f32[128,64]{0,1:T(8,128)S(1)}, f32[128,64]{0,1:T(8,128)S(1)}, u32[]{:S(2)}, u32[]{:S(2)}) collective-permute-start(f32[128,64]{0,1:T(8,128)S(1)} %get-tuple-element.36), channel_id=1, source_target_pairs={{0,12},{4,8},{8,4},{12,0},{1,13},{5,9},{9,5},{13,1},{2,14},{6,10},... | collective-permute-start | bytes 98312 | tf_op jit(solution)/shard_map/ppermute | solution.py:13
  125.3 13.9 %collective-permute-start.24 = (bf16[1,256,1024]{2,1,0:T(8,128)(2,1)S(1)}, bf16[1,256,1024]{2,1,0:T(8,128)(2,1)S(1)}, u32[]{:S(2)}, u32[]{:S(2)}) collective-permute-start(bf16[1,256,1024]{2,1,0:T(8,128)(2,1)S(1)} %fusion.24), channel_id=1, source_target_pairs={{0,2},{1,3},{2,0},{3,1},{4,6},{5,7},{6,4},{7,5},{8,10},{9,11},{10,... | collective-permute-start | bytes 1572872 | tf_op jit(solution)/shard_map/ppermute | solution.py:13
  129.3 18.6 %collective-permute-start.33 = (bf16[2,256,1024]{2,1,0:T(8,128)(2,1)S(1)}, bf16[2,256,1024]{2,1,0:T(8,128)(2,1)S(1)}, u32[]{:S(2)}, u32[]{:S(2)}) collective-permute-start(bf16[2,256,1024]{2,1,0:T(8,128)(2,1)S(1)} %bitcast.205), channel_id=1, source_target_pairs={{0,1},{1,0},{2,3},{3,2},{4,5},{5,4},{6,7},{7,6},{8,9},{9,8},{10,11... | collective-permute-start | bytes 3145736 | tf_op jit(solution)/shard_map/ppermute | solution.py:13
  139.5 8.3 %collective-permute-start.25 = (bf16[64,1024]{1,0:T(8,128)(2,1)S(1)}, bf16[64,1024]{1,0:T(8,128)(2,1)S(1)}, u32[]{:S(2)}, u32[]{:S(2)}) collective-permute-start(bf16[64,1024]{1,0:T(8,128)(2,1)S(1)} %get-tuple-element.32), channel_id=1, source_target_pairs={{0,4},{4,0},{8,12},{12,8},{1,5},{5,1},{9,13},{13,9},{2,6},{6,2},{1... | collective-permute-start | bytes 393224 | tf_op jit(solution)/shard_map/ppermute | solution.py:13
  139.8 13.1 %collective-permute-start.26 = (bf16[64,1024]{1,0:T(8,128)(2,1)S(1)}, bf16[64,1024]{1,0:T(8,128)(2,1)S(1)}, u32[]{:S(2)}, u32[]{:S(2)}) collective-permute-start(bf16[64,1024]{1,0:T(8,128)(2,1)S(1)} %get-tuple-element.31), channel_id=1, source_target_pairs={{0,8},{4,12},{8,0},{12,4},{1,9},{5,13},{9,1},{13,5},{2,10},{6,14},... | collective-permute-start | bytes 393224 | tf_op jit(solution)/shard_map/ppermute | solution.py:13
  141.8 12.4 %collective-permute-start.27 = (bf16[64,1024]{1,0:T(8,128)(2,1)S(1)}, bf16[64,1024]{1,0:T(8,128)(2,1)S(1)}, u32[]{:S(2)}, u32[]{:S(2)}) collective-permute-start(bf16[64,1024]{1,0:T(8,128)(2,1)S(1)} %get-tuple-element.30), channel_id=1, source_target_pairs={{0,12},{4,8},{8,4},{12,0},{1,13},{5,9},{9,5},{13,1},{2,14},{6,10},... | collective-permute-start | bytes 393224 | tf_op jit(solution)/shard_map/ppermute | solution.py:13
  144.3 18.2 %collective-permute-start.30 = (bf16[64,1024]{1,0:T(8,128)(2,1)S(1)}, bf16[64,1024]{1,0:T(8,128)(2,1)S(1)}, u32[]{:S(2)}, u32[]{:S(2)}) collective-permute-start(bf16[64,1024]{1,0:T(8,128)(2,1)S(1)} %get-tuple-element.29), channel_id=1, source_target_pairs={{0,4},{4,0},{8,12},{12,8},{1,5},{5,1},{9,13},{13,9},{2,6},{6,2},{1... | collective-permute-start | bytes 393224 | tf_op jit(solution)/shard_map/ppermute | solution.py:13
  147.8 15.5 %collective-permute-start.31 = (bf16[64,1024]{1,0:T(8,128)(2,1)S(1)}, bf16[64,1024]{1,0:T(8,128)(2,1)S(1)}, u32[]{:S(2)}, u32[]{:S(2)}) collective-permute-start(bf16[64,1024]{1,0:T(8,128)(2,1)S(1)} %get-tuple-element.28), channel_id=1, source_target_pairs={{0,8},{4,12},{8,0},{12,4},{1,9},{5,13},{9,1},{13,5},{2,10},{6,14},... | collective-permute-start | bytes 393224 | tf_op jit(solution)/shard_map/ppermute | solution.py:13
  147.9 23.8 %collective-permute-start.32 = (bf16[64,1024]{1,0:T(8,128)(2,1)S(1)}, bf16[64,1024]{1,0:T(8,128)(2,1)S(1)}, u32[]{:S(2)}, u32[]{:S(2)}) collective-permute-start(bf16[64,1024]{1,0:T(8,128)(2,1)S(1)} %get-tuple-element.27), channel_id=1, source_target_pairs={{0,12},{4,8},{8,4},{12,0},{1,13},{5,9},{9,5},{13,1},{2,14},{6,10},... | collective-permute-start | bytes 393224 | tf_op jit(solution)/shard_map/ppermute | solution.py:13
  152.9 9.2 %collective-permute-start.34 = (bf16[1,256,1024]{2,1,0:T(8,128)(2,1)S(1)}, bf16[1,256,1024]{2,1,0:T(8,128)(2,1)S(1)}, u32[]{:S(2)}, u32[]{:S(2)}) collective-permute-start(bf16[1,256,1024]{2,1,0:T(8,128)(2,1)S(1)} %fusion.26), channel_id=1, source_target_pairs={{0,2},{1,3},{2,0},{3,1},{4,6},{5,7},{6,4},{7,5},{8,10},{9,11},{10,... | collective-permute-start | bytes 1572872 | tf_op jit(solution)/shard_map/ppermute | solution.py:13
  162.3 7.5 %collective-permute-start.35 = (bf16[2,64,1024]{2,1,0:T(8,128)(2,1)S(1)}, bf16[2,64,1024]{2,1,0:T(8,128)(2,1)S(1)}, u32[]{:S(2)}, u32[]{:S(2)}) collective-permute-start(bf16[2,64,1024]{2,1,0:T(8,128)(2,1)S(1)} %fusion.35), channel_id=1, source_target_pairs={{0,4},{4,0},{8,12},{12,8},{1,5},{5,1},{9,13},{13,9},{2,6},{6,2},{1... | collective-permute-start | bytes 786440 | tf_op jit(solution)/shard_map/ppermute | solution.py:13
  169.9 7.3 %collective-permute-start.36 = (bf16[1,64,1024]{2,1,0:T(8,128)(2,1)S(1)}, bf16[1,64,1024]{2,1,0:T(8,128)(2,1)S(1)}, u32[]{:S(2)}, u32[]{:S(2)}) collective-permute-start(bf16[1,64,1024]{2,1,0:T(8,128)(2,1)S(1)} %fusion.43), channel_id=1, source_target_pairs={{0,8},{4,12},{8,0},{12,4},{1,9},{5,13},{9,1},{13,5},{2,10},{6,14},... | collective-permute-start | bytes 393224 | tf_op jit(solution)/shard_map/ppermute | solution.py:13
  171.7 6.3 %copy-start.2 = (f32[64,8192]{1,0:T(8,128)}, f32[64,8192]{1,0:T(8,128)S(1)}, u32[]{:S(2)}) copy-start(f32[64,8192]{1,0:T(8,128)S(1)} %convert_dynamic-update-slice_fusion) | copy-start | bytes 6291460

commit v2 on v1

--- a/solution.py
+++ b/solution.py
@@ -1,6 +1,8 @@
 import jax
 import jax.numpy as jnp
 from jax import lax
+from jax.experimental import pallas as pl
+from jax.experimental.pallas import tpu as pltpu
 from jax.sharding import PartitionSpec as P
 
 adapter_scale = 0.5
@@ -13,14 +15,16 @@
     return lax.ppermute(a, axis, [(i, i ^ bits) for i in range(n)])
 
 
-def gather(a, axis):
+def gather(a, axis, first=None):
     held = a[None]
     bit = lax.axis_size(axis) // 2
     while bit:
-        got = swap(held, axis, bit)
+        got = swap(held, axis, bit) if first is None or held.shape[0] > 1 else first
+        if held.shape[0] == 1:
+            first = got
         held = jnp.stack([held, got], 1).reshape((-1,) + a.shape)
         bit //= 2
-    return held
+    return held, first, got
 
 
 def exchange(pieces, axis):
@@ -43,13 +47,65 @@
     return scatter(pairs[:, 0], pairs[:, 1].astype(bf16), axis)
 
 
-def cut(a, size, start):
+any_space = pl.BlockSpec(memory_space=pl.ANY)
+hbm_space = pl.BlockSpec(memory_space=pltpu.HBM)
+
+
+def cut(a, size, start, *others):
     n_f = lax.axis_size("fsdp")
     depth = a.shape[1] // n_f
-    f = lax.axis_index("fsdp")
-    return [
-        lax.dynamic_slice_in_dim(a, (f ^ n) * depth + start, size, 1) for n in range(n_f)
-    ]
+
+    def body(index, source, *refs):
+        outs, (held, sem_in, sem_out) = refs[len(others) : -3], refs[-3:]
+        loads, stores = [], []
+        for n in range(n_f):
+            at = pl.multiple_of((index[0] ^ n) * depth + start, 128)
+            loads.append(
+                pltpu.make_async_copy(source.at[:, pl.ds(at, size)], held.at[n], sem_in.at[n])
+            )
+            stores.append(pltpu.make_async_copy(held.at[n], outs[n], sem_out.at[n]))
+        for load in loads:
+            load.start()
+        for load, store in zip(loads, stores):
+            load.wait()
+            store.start()
+        for store in stores:
+            store.wait()
+
+    return pl.pallas_call(
+        body,
+        out_shape=[jax.ShapeDtypeStruct((a.shape[0], size), a.dtype)] * n_f,
+        in_specs=[pl.BlockSpec(memory_space=pltpu.SMEM)] + [any_space] + [hbm_space] * len(others),
+        out_specs=[any_space] * n_f,
+        scratch_shapes=[
+            pltpu.VMEM((n_f, a.shape[0], size), a.dtype),
+            pltpu.SemaphoreType.DMA((n_f,)),
+            pltpu.SemaphoreType.DMA((n_f,)),
+        ],
+        cost_estimate=pl.CostEstimate(
+            flops=0, bytes_accessed=2 * n_f * a.shape[0] * size * 2, transcendentals=0
+        ),
+    )(lax.axis_index("fsdp")[None], a, *others)
+
+
+def copied(a, *others):
+    flat = a.reshape(-1, a.shape[-1])
+    rows = min(512, flat.shape[0])
+
+    def body(source, *refs):
+        refs[-1][...] = source[...]
+
+    block = pl.BlockSpec((rows, flat.shape[1]), lambda i: (i, 0))
+    return pl.pallas_call(
+        body,
+        grid=(flat.shape[0] // rows,),
+        out_shape=jax.ShapeDtypeStruct(flat.shape, a.dtype),
+        in_specs=[block] + [hbm_space] * len(others),
+        out_specs=block,
+        cost_estimate=pl.CostEstimate(
+            flops=0, bytes_accessed=4 * a.size, transcendentals=0
+        ),
+    )(flat, *others).reshape(a.shape)
 
 
 def dot(a, b, da, db):
@@ -98,11 +154,14 @@
     even_ids = adapters[0::2].reshape(-1)
     odd_ids = adapters[1::2].reshape(-1)
 
-    up_own = gather(up, "fsdp")
-    down_pieces = exchange(cut(down_t, depth, 0), "fsdp")
+    up_first = swap(up[None], "fsdp", n_f // 2)
+    up_own, _, _ = gather(up, "fsdp", up_first)
+    up_all, up_across, up_last = gather(up_own, "rows")
+    up_all = up_all.reshape(owners * rank, outputs)
+    down_pieces = exchange(cut(down_t, depth, 0, up_first), "fsdp")
     down_own = jnp.stack(down_pieces)
-    up_all = gather(up_own, "rows").reshape(owners * rank, outputs)
-    down_all = gather(down_own, "rows").reshape(owners * rank, depth)
+    down_all, _, _ = gather(down_own, "rows")
+    down_all = down_all.reshape(owners * rank, depth)
 
     back = (adapter_scale * pick(dot(output_gradient, up_all, 1, 1), ids, all_ids)).astype(bf16)
     packed = jnp.concatenate(
@@ -134,8 +193,11 @@
     base = 0.0
     hidden_part = 0.0
     grad_pieces = []
+    cut_after = [(down_pieces[n_f // 2],), ()]
     for c in range(chunks):
-        x_pieces = exchange(cut(rollout, part, c * part), "fsdp")
+        x_pieces = exchange(cut(rollout, part, c * part, *cut_after[c]), "fsdp")
+        if c + 1 < chunks:
+            cut_after[c + 1] += (x_pieces[n_f // 2],)
         x_part = jnp.concatenate(x_pieces, 0)
         odd = dot(back_odd, x_part, 0, 0).astype(bf16).reshape(n_r // 2, n_f * rank, part)
         even = dot(back_even, x_part, 0, 0).reshape(n_r // 2, n_f * rank, part)
@@ -157,15 +219,22 @@
         odd.astype(bf16).reshape(n_r // 2, n_f * rank, outputs),
         "rows",
     )
-    up_grad = scatter_all(up_grad.reshape(n_f, rank, outputs), "fsdp")
-
+    down_moved = []
+    for c in range(chunks):
+        piece = grad_pieces[c].reshape(n_f, rank, part)
+        down_moved.append(
+            exchange([piece[0]] + [piece[n].astype(bf16) for n in range(1, n_f)], "fsdp")
+        )
     grad_down = jnp.zeros((rank, width), f32)
     for c in range(chunks):
-        piece = grad_pieces[c].reshape(n_f, rank, part)
-        got = exchange([piece[0]] + [piece[n].astype(bf16) for n in range(1, n_f)], "fsdp")
         for n in range(n_f):
             at = (f ^ n) * depth + c * part
-            grad_down = lax.dynamic_update_slice_in_dim(grad_down, got[n].astype(f32), at, 1)
+            got = down_moved[c][n].astype(f32)
+            grad_down = lax.dynamic_update_slice_in_dim(grad_down, got, at, 1)
+    pairs = up_grad.reshape(n_f // 2, 2, rank, outputs)
+    odd = copied(pairs[:, 1].astype(bf16), down_moved[0][n_f // 2])
+    up_grad = scatter(pairs[:, 0], odd, "fsdp")
+
     return (mixed, jnp.swapaxes(grad_down, 0, 1)[None], up_grad[None])
 
 

time: 178 us -> 174 us (0.978)
  waiting for transfers between devices: 110 us -> 83.5 us
  Pallas kernels: 0 us -> 7.58 us
  other arithmetic: 6.64 us -> 13.7 us
  local copies, waits for them, and re-layouts: 4.54 us -> 8.31 us
  starting transfers between devices: 45.2 us -> 48 us
    ppermute x37, waiting for transfers between devices: 110 us -> 83.5 us  [swap(): return lax.ppermute(a, axis, [(i, i ^ bits) for i in range(n)])]
    pallas_call x0 -> x4, Pallas kernels: none -> 7.58 us  [the longest x3 5.91 us: cut(): pl.pallas_call(body, out_shape=[jax.ShapeDtypeStruct((a.shape[0], size),...]
    unnamed x16 -> x24, local copies, waits for them, and re-layouts: 0.04 us -> 4.1 us
    another operation x7, other arithmetic: 3.33 us -> 6.59 us  [gather(): held = jnp.stack([held, got], 1).reshape((-1,) + a.shape)]
    ppermute x37, starting transfers between devices: 45.2 us -> 48 us  [swap(): return lax.ppermute(a, axis, [(i, i ^ bits) for i in range(n)])]
    another operation x1 -> x0, local copies, waits for them, and re-layouts: 2.26 us -> none  [per_device(): down_own = jnp.stack(down_pieces)]
    dynamic_update_slice x6, other arithmetic: 0.13 us -> 1.94 us  [per_device(): grad_down = lax.dynamic_update_slice_in_dim(grad_down, got, at, 1)]
  transfers between devices with their start and end apart: 37 -> 37, of which waited for: 17 -> 15; matrix products, arithmetic and copies ran while one was open for 11% -> 17% of each run, Pallas kernels for 0% -> 3%
where the time goes in v2:
time: 174 us; the launch traced here: 173 us
  waiting for transfers between devices  83.5 us (48%)
  starting transfers between devices  48 us (28%)
  other arithmetic  13.7 us (8%)
  matrix products  10.8 us (6%)
  local copies, waits for them, and re-layouts  8.31 us (5%)
  Pallas kernels  7.58 us (4%)
    ppermute x37, waiting for transfers between devices, swap(): return lax.ppermute(a, axis, [(i, i ^ bits) for i in range(n)])  83.5 us
    ppermute x37, starting transfers between devices, swap(): return lax.ppermute(a, axis, [(i, i ^ bits) for i in range(n)])  48 us
    dot_general x12, matrix products, dot(): lax.dot_general(a, b, (((da,), (db,)), ((), ())), preferred_element_type=...  10.8 us
    another operation x7, other arithmetic, gather(): held = jnp.stack([held, got], 1).reshape((-1,) + a.shape)  6.59 us
    pallas_call x3, Pallas kernels, cut(): pl.pallas_call(body, out_shape=[jax.ShapeDtypeStruct((a.shape[0], size),...  5.91 us
    unnamed x24, local copies, waits for them, and re-layouts  4.1 us
  transfers between devices with their start and end apart: 37, of which 15 were waited for; matrix products, arithmetic and copies ran while one was open for 17% of the time, Pallas kernels for 3%

profile of v2, /device:TPU:0, one launch (start us, length us, event | category | flops | bytes accessed | tf_op | source)
XLA Modules:
  0.0 173.3 jit_solution(6866688509378348285)
XLA Ops:
  0.6 4.1 %collective-permute-start = (bf16[1,64,1024]{2,1,0:T(8,128)(2,1)}, bf16[1,64,1024]{2,1,0:T(8,128)(2,1)S(1)}, u32[]{:S(2)}, u32[]{:S(2)}) collective-permute-start(bf16[1,64,1024]{2,1,0:T(8,128)(2,1)} %param.10), channel_id=1, source_target_pairs={{0,8},{4,12},{8,0},{12,4},{1,9},{5,13},{9,1},{13,5},{2,10},{6,14},... | collective-permute-start | bytes 393224 | tf_op jit(solution)/shard_map/ppermute | solution.py:15
  5.1 0.7 broadcast_compare_fusion.4
  5.9 0.7 broadcast_compare_fusion.3
  6.6 4.7 %collective-permute-done.refs_0_ = bf16[1,64,1024]{2,1,0:T(8,128)(2,1)S(1)} collective-permute-done((bf16[1,64,1024]{2,1,0:T(8,128)(2,1)}, bf16[1,64,1024]{2,1,0:T(8,128)(2,1)S(1)}, u32[]{:S(2)}, u32[]{:S(2)}) %collective-permute-start) | collective-permute-done | bytes 131104 | tf_op jit(solution)/shard_map/ppermute | solution.py:15
  11.9 2.0 %shard_map.88 = (bf16[64,2048]{1,0:T(8,128)(2,1)}, bf16[64,2048]{1,0:T(8,128)(2,1)}, bf16[64,2048]{1,0:T(8,128)(2,1)}, bf16[64,2048]{1,0:T(8,128)(2,1)}) custom-call(s32[1]{0:T(128)} %bitcast.index, bf16[64,8192]{1,0:T(8,128)(2,1)} %bitcast.195, bf16[1,64,1024]{2,1,0:T(8,128)(2,1)} %copy-done.5), custom_call_target="tpu_custom_call" | custom-call | bytes 2097152 | tf_op jit(solution)/shard_map/pallas_call | solution.py:75
  14.0 4.1 %collective-permute-start.16 = (bf16[64,2048]{1,0:T(8,128)(2,1)}, bf16[64,2048]{1,0:T(8,128)(2,1)S(1)}, u32[]{:S(2)}, u32[]{:S(2)}) collective-permute-start(bf16[64,2048]{1,0:T(8,128)(2,1)} %get-tuple-element.25), channel_id=1, source_target_pairs={{0,4},{4,0},{8,12},{12,8},{1,5},{5,1},{9,13},{13,9},{2,6},{6,2},{1... | collective-permute-start | bytes 786440 | tf_op jit(solution)/shard_map/ppermute | solution.py:15
  18.4 1.0 fusion.41
  19.8 0.7 convert_bitcast_fusion
  20.4 14.6 %collective-permute-done.1.refs_0_ = bf16[64,2048]{1,0:T(8,128)(2,1)S(1)} collective-permute-done((bf16[64,2048]{1,0:T(8,128)(2,1)}, bf16[64,2048]{1,0:T(8,128)(2,1)S(1)}, u32[]{:S(2)}, u32[]{:S(2)}) %collective-permute-start.1) | collective-permute-done | bytes 262176 | tf_op jit(solution)/shard_map/ppermute | solution.py:15
  35.1 0.7 copy-done.2
  35.8 2.0 %shard_map.89 = (bf16[128,1024]{1,0:T(8,128)(2,1)}, bf16[128,1024]{1,0:T(8,128)(2,1)}, bf16[128,1024]{1,0:T(8,128)(2,1)}, bf16[128,1024]{1,0:T(8,128)(2,1)}) custom-call(s32[1]{0:T(128)} %bitcast.index, bf16[128,8192]{1,0:T(8,128)(2,1)} %source.3, bf16[64,2048]{1,0:T(8,128)(2,1)} %copy-done.2), custom_call_target="tpu_custom_call" | custom-call | bytes 2097152 | tf_op jit(solution)/shard_map/pallas_call | solution.py:75
  37.9 2.1 %fusion.39 = (bf16[1,1,4,64,2048]{4,3,2,1,0:T(8,128)(2,1)S(1)}, bf16[1,4,64,2048]{3,2,1,0:T(8,128)(2,1)}) fusion(bf16[1,64,2048]{2,1,0:T(8,128)(2,1)S(1)} %bitcast.207, bf16[1,64,2048]{2,1,0:T(8,128)(2,1)} %bitcast.194, bf16[1,64,2048]{2,1,0:T(8,128)(2,1)S(1)} %bitcast.206, bf16[1,64,2048]{2,1,0:T(8,128)(2,1)S(1)} %bitcast.205), kind=kLoop, calls=%fused_computation.80 | loop fusion | flops 1572864 | bytes 3145728 | tf_op jit(solution)/shard_map/stack;broadcast_in_dim | solution.py:25
  40.0 1.6 collective-permute-start.18
  41.6 8.9 %collective-permute-start.2 = (bf16[128,1024]{1,0:T(8,128)(2,1)}, bf16[128,1024]{1,0:T(8,128)(2,1)S(1)}, u32[]{:S(2)}, u32[]{:S(2)}) collective-permute-start(bf16[128,1024]{1,0:T(8,128)(2,1)} %get-tuple-element.17), channel_id=1, source_target_pairs={{0,4},{4,0},{8,12},{12,8},{1,5},{5,1},{9,13},{13,9},{2,6},{6,2},{1... | collective-permute-start | bytes 786440 | tf_op jit(solution)/shard_map/ppermute | solution.py:15
  50.8 4.6 %collective-permute-done.3.refs_0_ = bf16[128,1024]{1,0:T(8,128)(2,1)S(1)} collective-permute-done((bf16[128,1024]{1,0:T(8,128)(2,1)}, bf16[128,1024]{1,0:T(8,128)(2,1)S(1)}, u32[]{:S(2)}, u32[]{:S(2)}) %collective-permute-start.3) | collective-permute-done | bytes 262176 | tf_op jit(solution)/shard_map/ppermute | solution.py:15
  55.4 0.7 copy-done.3
  56.1 2.0 %shard_map.90 = (bf16[128,1024]{1,0:T(8,128)(2,1)}, bf16[128,1024]{1,0:T(8,128)(2,1)}, bf16[128,1024]{1,0:T(8,128)(2,1)}, bf16[128,1024]{1,0:T(8,128)(2,1)}) custom-call(s32[1]{0:T(128)} %bitcast.index, bf16[128,8192]{1,0:T(8,128)(2,1)} %source.3, bf16[128,1024]{1,0:T(8,128)(2,1)} %copy-done.3), custom_call_target="tpu_custom_call" | custom-call | bytes 2097152 | tf_op jit(solution)/shard_map/pallas_call | solution.py:75
  58.1 1.0 constant_dynamic-update-slice_fusion.7
  59.1 2.7 %collective-permute-done.2 = bf16[128,1024]{1,0:T(8,128)(2,1)S(1)} collective-permute-done((bf16[128,1024]{1,0:T(8,128)(2,1)}, bf16[128,1024]{1,0:T(8,128)(2,1)S(1)}, u32[]{:S(2)}, u32[]{:S(2)}) %collective-permute-start.2) | collective-permute-done | bytes 262176 | tf_op jit(solution)/shard_map/ppermute | solution.py:15
  61.8 1.0 constant_dynamic-update-slice_fusion.1
  62.8 2.1 %collective-permute-start.7 = (bf16[128,1024]{1,0:T(8,128)(2,1)}, bf16[128,1024]{1,0:T(8,128)(2,1)S(1)}, u32[]{:S(2)}, u32[]{:S(2)}) collective-permute-start(bf16[128,1024]{1,0:T(8,128)(2,1)} %get-tuple-element.23), channel_id=1, source_target_pairs={{0,12},{4,8},{8,4},{12,0},{1,13},{5,9},{9,5},{13,1},{2,14},{6,10},... | collective-permute-start | bytes 786440 | tf_op jit(solution)/shard_map/ppermute | solution.py:15
  65.0 1.0 constant_dynamic-update-slice_fusion
  65.9 7.8 %collective-permute-done.11 = bf16[1,4,64,1024]{3,2,1,0:T(8,128)(2,1)} collective-permute-done((bf16[1,4,64,1024]{3,2,1,0:T(8,128)(2,1)S(1)}, bf16[1,4,64,1024]{3,2,1,0:T(8,128)(2,1)}, u32[]{:S(2)}, u32[]{:S(2)}) %collective-permute-start.11) | collective-permute-done | bytes 524320 | tf_op jit(solution)/shard_map/ppermute | solution.py:15
  73.8 1.3 fusion.23
  75.2 6.8 %collective-permute-done.6 = bf16[128,1024]{1,0:T(8,128)(2,1)S(1)} collective-permute-done((bf16[128,1024]{1,0:T(8,128)(2,1)}, bf16[128,1024]{1,0:T(8,128)(2,1)S(1)}, u32[]{:S(2)}, u32[]{:S(2)}) %collective-permute-start.6) | collective-permute-done | bytes 262176 | tf_op jit(solution)/shard_map/ppermute | solution.py:15
  82.1 1.3 fusion.4
  83.3 1.3 fusion.8
  84.7 3.6 %collective-permute-start.8 = (bf16[2,128,1024]{2,1,0:T(8,128)(2,1)S(1)}, bf16[2,128,1024]{2,1,0:T(8,128)(2,1)S(1)}, u32[]{:S(2)}, u32[]{:S(2)}) collective-permute-start(bf16[2,128,1024]{2,1,0:T(8,128)(2,1)S(1)} %fusion.27), channel_id=1, source_target_pairs={{0,4},{4,0},{8,12},{12,8},{1,5},{5,1},{9,13},{13,9},{2,6},{6,2},{1... | collective-permute-start | bytes 1572872 | tf_op jit(solution)/shard_map/ppermute | solution.py:15
  88.8 0.7 fusion.51
  89.7 3.8 %collective-permute-start.14 = (bf16[128,128]{0,1:T(8,128)(2,1)S(1)}, bf16[128,128]{0,1:T(8,128)(2,1)S(1)}, u32[]{:S(2)}, u32[]{:S(2)}) collective-permute-start(bf16[128,128]{0,1:T(8,128)(2,1)S(1)} %pad_maximum_fusion.11), channel_id=1, source_target_pairs={{0,8},{4,12},{8,0},{12,4},{1,9},{5,13},{9,1},{13,5},{2,10},{6,14},... | collective-permute-start | bytes 98312 | tf_op jit(solution)/shard_map/ppermute | solution.py:15
  94.1 1.5 fusion.12
  95.7 5.6 %collective-permute-done.13 = bf16[128,128]{0,1:T(8,128)(2,1)S(1)} collective-permute-done((bf16[128,128]{0,1:T(8,128)(2,1)S(1)}, bf16[128,128]{0,1:T(8,128)(2,1)S(1)}, u32[]{:S(2)}, u32[]{:S(2)}) %collective-permute-start.13) | collective-permute-done | bytes 32800 | tf_op jit(solution)/shard_map/ppermute | solution.py:15
  101.3 3.7 %collective-permute-done.15 = bf16[128,128]{0,1:T(8,128)(2,1)S(1)} collective-permute-done((bf16[128,128]{0,1:T(8,128)(2,1)S(1)}, bf16[128,128]{0,1:T(8,128)(2,1)S(1)}, u32[]{:S(2)}, u32[]{:S(2)}) %collective-permute-start.15) | collective-permute-done | bytes 32800 | tf_op jit(solution)/shard_map/ppermute | solution.py:15
  105.2 0.7 convolution_convert_fusion.1
  106.0 0.7 convolution_convert_fusion
  107.6 1.0 collective-permute-done.23
  108.6 0.7 add_bitcast_fusion.2
  109.5 0.7 collective-permute-start.24
  110.1 0.7 add_bitcast_fusion.1
  111.9 1.3 fusion.2
  113.2 1.3 fusion
  114.5 0.7 select_reduce_fusion
  115.5 1.9 %collective-permute-start.21 = (f32[128,64]{0,1:T(8,128)S(1)}, f32[128,64]{0,1:T(8,128)S(1)}, u32[]{:S(2)}, u32[]{:S(2)}) collective-permute-start(f32[128,64]{0,1:T(8,128)S(1)} %get-tuple-element.49), channel_id=1, source_target_pairs={{0,8},{4,12},{8,0},{12,4},{1,9},{5,13},{9,1},{13,5},{2,10},{6,14},... | collective-permute-start | bytes 98312 | tf_op jit(solution)/shard_map/ppermute | solution.py:15
  117.4 2.3 %collective-permute-start.22 = (f32[128,64]{0,1:T(8,128)S(1)}, f32[128,64]{0,1:T(8,128)S(1)}, u32[]{:S(2)}, u32[]{:S(2)}) collective-permute-start(f32[128,64]{0,1:T(8,128)S(1)} %get-tuple-element.48), channel_id=1, source_target_pairs={{0,12},{4,8},{8,4},{12,0},{1,13},{5,9},{9,5},{13,1},{2,14},{6,10},... | collective-permute-start | bytes 98312 | tf_op jit(solution)/shard_map/ppermute | solution.py:15
  119.7 1.8 %collective-permute-done.20 = f32[128,64]{0,1:T(8,128)S(1)} collective-permute-done((f32[128,64]{0,1:T(8,128)S(1)}, f32[128,64]{0,1:T(8,128)S(1)}, u32[]{:S(2)}, u32[]{:S(2)}) %collective-permute-start.20) | collective-permute-done | bytes 32800 | tf_op jit(solution)/shard_map/ppermute | solution.py:15
  121.5 1.5 collective-permute-start.29
  123.0 1.2 collective-permute-done.21
  125.0 1.6 collective-permute-start.26
  127.4 8.0 %collective-permute-done.29 = bf16[1,256,1024]{2,1,0:T(8,128)(2,1)S(1)} collective-permute-done((bf16[1,256,1024]{2,1,0:T(8,128)(2,1)S(1)}, bf16[1,256,1024]{2,1,0:T(8,128)(2,1)S(1)}, u32[]{:S(2)}, u32[]{:S(2)}) %collective-permute-start.29) | collective-permute-done | bytes 524320 | tf_op jit(solution)/shard_map/ppermute | solution.py:15
  135.4 1.6 collective-permute-start.27
  137.2 0.8 slice_bitcast_fusion.8
  138.0 1.2 fusion.33
  139.4 2.8 %collective-permute-start.31 = (bf16[64,1024]{1,0:T(8,128)(2,1)}, bf16[64,1024]{1,0:T(8,128)(2,1)}, u32[]{:S(2)}, u32[]{:S(2)}) collective-permute-start(bf16[64,1024]{1,0:T(8,128)(2,1)} %get-tuple-element.40), channel_id=1, source_target_pairs={{0,8},{4,12},{8,0},{12,4},{1,9},{5,13},{9,1},{13,5},{2,10},{6,14},... | collective-permute-start | bytes 393224 | tf_op jit(solution)/shard_map/ppermute | solution.py:15
  142.2 1.7 collective-permute-start.32
  144.5 1.2 collective-permute-start.34
  145.8 10.6 %collective-permute-done.34 = bf16[1,256,1024]{2,1,0:T(8,128)(2,1)S(1)} collective-permute-done((bf16[1,256,1024]{2,1,0:T(8,128)(2,1)S(1)}, bf16[1,256,1024]{2,1,0:T(8,128)(2,1)S(1)}, u32[]{:S(2)}, u32[]{:S(2)}) %collective-permute-start.34) | collective-permute-done | bytes 524320 | tf_op jit(solution)/shard_map/ppermute | solution.py:15
  156.6 0.7 slice.233
  157.3 1.7 shard_map.91
  159.0 0.9 convert_dynamic-update-slice_fusion.1
  160.0 6.0 %collective-permute-done.35 = bf16[2,64,1024]{2,1,0:T(8,128)(2,1)S(1)} collective-permute-done((bf16[2,64,1024]{2,1,0:T(8,128)(2,1)}, bf16[2,64,1024]{2,1,0:T(8,128)(2,1)S(1)}, u32[]{:S(2)}, u32[]{:S(2)}) %collective-permute-start.35) | collective-permute-done | bytes 262176 | tf_op jit(solution)/shard_map/ppermute | solution.py:15
  166.0 1.2 collective-permute-start.36
  167.3 0.9 convert_dynamic-update-slice_fusion
  168.2 4.4 %collective-permute-done.36 = bf16[1,64,1024]{2,1,0:T(8,128)(2,1)S(1)} collective-permute-done((bf16[1,64,1024]{2,1,0:T(8,128)(2,1)S(1)}, bf16[1,64,1024]{2,1,0:T(8,128)(2,1)S(1)}, u32[]{:S(2)}, u32[]{:S(2)}) %collective-permute-start.36) | collective-permute-done | bytes 131104 | tf_op jit(solution)/shard_map/ppermute | solution.py:15
  172.6 0.7 fusion.35
  (112 shorter events, 9.1 us)
Async XLA Ops:
  0.6 88.2 %copy-start = (bf16[128,1024]{1,0:T(8,128)(2,1)S(1)}, bf16[128,1024]{1,0:T(8,128)(2,1)}, u32[]{:S(2)}) copy-start(bf16[128,1024]{1,0:T(8,128)(2,1)} %param.11) | copy-start | bytes 786436
  0.6 10.6 %collective-permute-start = (bf16[1,64,1024]{2,1,0:T(8,128)(2,1)}, bf16[1,64,1024]{2,1,0:T(8,128)(2,1)S(1)}, u32[]{:S(2)}, u32[]{:S(2)}) collective-permute-start(bf16[1,64,1024]{2,1,0:T(8,128)(2,1)} %param.10), channel_id=1, source_target_pairs={{0,8},{4,12},{8,0},{12,4},{1,9},{5,13},{9,1},{13,5},{2,10},{6,14},... | collective-permute-start | bytes 393224 | tf_op jit(solution)/shard_map/ppermute | solution.py:15
  11.3 0.7 copy-start.5
  13.9 24.0 %copy-start.6 = (bf16[64,2048]{1,0:T(8,128)(2,1)S(1)}, bf16[64,2048]{1,0:T(8,128)(2,1)}, u32[]{:S(2)}) copy-start(bf16[64,2048]{1,0:T(8,128)(2,1)} %get-tuple-element.24) | copy-start | bytes 786436
  13.9 21.2 %collective-permute-start.1 = (bf16[64,2048]{1,0:T(8,128)(2,1)}, bf16[64,2048]{1,0:T(8,128)(2,1)S(1)}, u32[]{:S(2)}, u32[]{:S(2)}) collective-permute-start(bf16[64,2048]{1,0:T(8,128)(2,1)} %get-tuple-element.15), channel_id=1, source_target_pairs={{0,8},{4,12},{8,0},{12,4},{1,9},{5,13},{9,1},{13,5},{2,10},{6,14},... | collective-permute-start | bytes 786440 | tf_op jit(solution)/shard_map/ppermute | solution.py:15
  14.0 23.9 %collective-permute-start.16 = (bf16[64,2048]{1,0:T(8,128)(2,1)}, bf16[64,2048]{1,0:T(8,128)(2,1)S(1)}, u32[]{:S(2)}, u32[]{:S(2)}) collective-permute-start(bf16[64,2048]{1,0:T(8,128)(2,1)} %get-tuple-element.25), channel_id=1, source_target_pairs={{0,4},{4,0},{8,12},{12,8},{1,5},{5,1},{9,13},{13,9},{2,6},{6,2},{1... | collective-permute-start | bytes 786440 | tf_op jit(solution)/shard_map/ppermute | solution.py:15
  18.1 19.8 %collective-permute-start.17 = (bf16[64,2048]{1,0:T(8,128)(2,1)}, bf16[64,2048]{1,0:T(8,128)(2,1)S(1)}, u32[]{:S(2)}, u32[]{:S(2)}) collective-permute-start(bf16[64,2048]{1,0:T(8,128)(2,1)} %get-tuple-element.26), channel_id=1, source_target_pairs={{0,12},{4,8},{8,4},{12,0},{1,13},{5,9},{9,5},{13,1},{2,14},{6,10},... | collective-permute-start | bytes 786440 | tf_op jit(solution)/shard_map/ppermute | solution.py:15
  19.4 31.2 %collective-permute-start.10 = (bf16[2,64,1024]{2,1,0:T(8,128)(2,1)S(1)}, bf16[2,64,1024]{2,1,0:T(8,128)(2,1)S(1)}, u32[]{:S(2)}, u32[]{:S(2)}) collective-permute-start(bf16[2,64,1024]{2,1,0:T(8,128)(2,1)S(1)} %get-tuple-element.46), channel_id=1, source_target_pairs={{0,4},{4,0},{8,12},{12,8},{1,5},{5,1},{9,13},{13,9},{2,6},{6,2},{1... | collective-permute-start | bytes 786440 | tf_op jit(solution)/shard_map/ppermute | solution.py:15
  35.1 0.7 copy-start.2
  37.8 17.6 %collective-permute-start.3 = (bf16[128,1024]{1,0:T(8,128)(2,1)}, bf16[128,1024]{1,0:T(8,128)(2,1)S(1)}, u32[]{:S(2)}, u32[]{:S(2)}) collective-permute-start(bf16[128,1024]{1,0:T(8,128)(2,1)} %get-tuple-element.18), channel_id=1, source_target_pairs={{0,8},{4,12},{8,0},{12,4},{1,9},{5,13},{9,1},{13,5},{2,10},{6,14},... | collective-permute-start | bytes 786440 | tf_op jit(solution)/shard_map/ppermute | solution.py:15
  37.9 12.8 %copy-start.7 = (bf16[128,1024]{1,0:T(8,128)(2,1)S(1)}, bf16[128,1024]{1,0:T(8,128)(2,1)}, u32[]{:S(2)}) copy-start(bf16[128,1024]{1,0:T(8,128)(2,1)} %get-tuple-element.16) | copy-start | bytes 786436
  40.0 54.1 %collective-permute-start.18 = (bf16[1,4,64,2048]{3,2,1,0:T(8,128)(2,1)}, bf16[1,4,64,2048]{3,2,1,0:T(8,128)(2,1)}, u32[]{:S(2)}, u32[]{:S(2)}) collective-permute-start(bf16[1,4,64,2048]{3,2,1,0:T(8,128)(2,1)} %get-tuple-element.38), channel_id=1, source_target_pairs={{0,2},{1,3},{2,0},{3,1},{4,6},{5,7},{6,4},{7,5},{8,10},{9,11},{10,... | collective-permute-start | bytes 3145736 | tf_op jit(solution)/shard_map/ppermute | solution.py:15
  41.6 20.2 %collective-permute-start.2 = (bf16[128,1024]{1,0:T(8,128)(2,1)}, bf16[128,1024]{1,0:T(8,128)(2,1)S(1)}, u32[]{:S(2)}, u32[]{:S(2)}) collective-permute-start(bf16[128,1024]{1,0:T(8,128)(2,1)} %get-tuple-element.17), channel_id=1, source_target_pairs={{0,4},{4,0},{8,12},{12,8},{1,5},{5,1},{9,13},{13,9},{2,6},{6,2},{1... | collective-permute-start | bytes 786440 | tf_op jit(solution)/shard_map/ppermute | solution.py:15
  50.6 23.2 %collective-permute-start.11 = (bf16[1,4,64,1024]{3,2,1,0:T(8,128)(2,1)S(1)}, bf16[1,4,64,1024]{3,2,1,0:T(8,128)(2,1)}, u32[]{:S(2)}, u32[]{:S(2)}) collective-permute-start(bf16[1,4,64,1024]{3,2,1,0:T(8,128)(2,1)S(1)} %bitcast.188), channel_id=1, source_target_pairs={{0,2},{1,3},{2,0},{3,1},{4,6},{5,7},{6,4},{7,5},{8,10},{9,11},{10,... | collective-permute-start | bytes 1572872 | tf_op jit(solution)/shard_map/ppermute | solution.py:15
  50.7 12.1 %collective-permute-start.4 = (bf16[128,1024]{1,0:T(8,128)(2,1)}, bf16[128,1024]{1,0:T(8,128)(2,1)}, u32[]{:S(2)}, u32[]{:S(2)}) collective-permute-start(bf16[128,1024]{1,0:T(8,128)(2,1)} %get-tuple-element.19), channel_id=1, source_target_pairs={{0,12},{4,8},{8,4},{12,0},{1,13},{5,9},{9,5},{13,1},{2,14},{6,10},... | collective-permute-start | bytes 786440 | tf_op jit(solution)/shard_map/ppermute | solution.py:15
  55.4 0.7 copy-start.3
  59.1 16.1 %collective-permute-start.5 = (bf16[128,1024]{1,0:T(8,128)(2,1)}, bf16[128,1024]{1,0:T(8,128)(2,1)S(1)}, u32[]{:S(2)}, u32[]{:S(2)}) collective-permute-start(bf16[128,1024]{1,0:T(8,128)(2,1)} %get-tuple-element.21), channel_id=1, source_target_pairs={{0,4},{4,0},{8,12},{12,8},{1,5},{5,1},{9,13},{13,9},{2,6},{6,2},{1... | collective-permute-start | bytes 786440 | tf_op jit(solution)/shard_map/ppermute | solution.py:15
  61.8 20.2 %collective-permute-start.6 = (bf16[128,1024]{1,0:T(8,128)(2,1)}, bf16[128,1024]{1,0:T(8,128)(2,1)S(1)}, u32[]{:S(2)}, u32[]{:S(2)}) collective-permute-start(bf16[128,1024]{1,0:T(8,128)(2,1)} %get-tuple-element.22), channel_id=1, source_target_pairs={{0,8},{4,12},{8,0},{12,4},{1,9},{5,13},{9,1},{13,5},{2,10},{6,14},... | collective-permute-start | bytes 786440 | tf_op jit(solution)/shard_map/ppermute | solution.py:15
  62.8 19.2 %collective-permute-start.7 = (bf16[128,1024]{1,0:T(8,128)(2,1)}, bf16[128,1024]{1,0:T(8,128)(2,1)S(1)}, u32[]{:S(2)}, u32[]{:S(2)}) collective-permute-start(bf16[128,1024]{1,0:T(8,128)(2,1)} %get-tuple-element.23), channel_id=1, source_target_pairs={{0,12},{4,8},{8,4},{12,0},{1,13},{5,9},{9,5},{13,1},{2,14},{6,10},... | collective-permute-start | bytes 786440 | tf_op jit(solution)/shard_map/ppermute | solution.py:15
  73.8 8.3 %copy-start.8 = (bf16[2048,1024]{1,0:T(8,128)(2,1)S(1)}, bf16[2048,1024]{1,0:T(8,128)(2,1)}, u32[]{:S(2)}) copy-start(bf16[2048,1024]{1,0:T(8,128)(2,1)} %param.8) | copy-start | bytes 12582916
  75.1 13.2 %collective-permute-start.12 = (bf16[2,4,64,1024]{3,2,1,0:T(8,128)(2,1)S(1)}, bf16[2,4,64,1024]{3,2,1,0:T(8,128)(2,1)S(1)}, u32[]{:S(2)}, u32[]{:S(2)}) collective-permute-start(bf16[2,4,64,1024]{3,2,1,0:T(8,128)(2,1)S(1)} %get-tuple-element.36), channel_id=1, source_target_pairs={{0,1},{1,0},{2,3},{3,2},{4,5},{5,4},{6,7},{7,6},{8,9},{9,8},{10,11... | collective-permute-start | bytes 3145736 | tf_op jit(solution)/shard_map/ppermute | solution.py:15
  84.7 22.6 %collective-permute-start.8 = (bf16[2,128,1024]{2,1,0:T(8,128)(2,1)S(1)}, bf16[2,128,1024]{2,1,0:T(8,128)(2,1)S(1)}, u32[]{:S(2)}, u32[]{:S(2)}) collective-permute-start(bf16[2,128,1024]{2,1,0:T(8,128)(2,1)S(1)} %fusion.27), channel_id=1, source_target_pairs={{0,4},{4,0},{8,12},{12,8},{1,5},{5,1},{9,13},{13,9},{2,6},{6,2},{1... | collective-permute-start | bytes 1572872 | tf_op jit(solution)/shard_map/ppermute | solution.py:15
  89.6 11.7 %collective-permute-start.13 = (bf16[128,128]{0,1:T(8,128)(2,1)S(1)}, bf16[128,128]{0,1:T(8,128)(2,1)S(1)}, u32[]{:S(2)}, u32[]{:S(2)}) collective-permute-start(bf16[128,128]{0,1:T(8,128)(2,1)S(1)} %pad_maximum_fusion.11), channel_id=1, source_target_pairs={{0,4},{4,0},{8,12},{12,8},{1,5},{5,1},{9,13},{13,9},{2,6},{6,2},{1... | collective-permute-start | bytes 98312 | tf_op jit(solution)/shard_map/ppermute | solution.py:15
  89.7 11.6 %collective-permute-start.14 = (bf16[128,128]{0,1:T(8,128)(2,1)S(1)}, bf16[128,128]{0,1:T(8,128)(2,1)S(1)}, u32[]{:S(2)}, u32[]{:S(2)}) collective-permute-start(bf16[128,128]{0,1:T(8,128)(2,1)S(1)} %pad_maximum_fusion.11), channel_id=1, source_target_pairs={{0,8},{4,12},{8,0},{12,4},{1,9},{5,13},{9,1},{13,5},{2,10},{6,14},... | collective-permute-start | bytes 98312 | tf_op jit(solution)/shard_map/ppermute | solution.py:15
  93.5 11.5 %collective-permute-start.15 = (bf16[128,128]{0,1:T(8,128)(2,1)S(1)}, bf16[128,128]{0,1:T(8,128)(2,1)S(1)}, u32[]{:S(2)}, u32[]{:S(2)}) collective-permute-start(bf16[128,128]{0,1:T(8,128)(2,1)S(1)} %pad_maximum_fusion.11), channel_id=1, source_target_pairs={{0,12},{4,8},{8,4},{12,0},{1,13},{5,9},{9,5},{13,1},{2,14},{6,10},... | collective-permute-start | bytes 98312 | tf_op jit(solution)/shard_map/ppermute | solution.py:15
  95.6 15.3 %collective-permute-start.19 = (bf16[2,4,64,2048]{3,2,1,0:T(8,128)(2,1)S(1)}, bf16[2,4,64,2048]{3,2,1,0:T(8,128)(2,1)S(1)}, u32[]{:S(2)}, u32[]{:S(2)}) collective-permute-start(bf16[2,4,64,2048]{3,2,1,0:T(8,128)(2,1)S(1)} %get-tuple-element.34), channel_id=1, source_target_pairs={{0,1},{1,0},{2,3},{3,2},{4,5},{5,4},{6,7},{7,6},{8,9},{9,8},{10,11... | collective-permute-start | bytes 6291464 | tf_op jit(solution)/shard_map/ppermute | solution.py:15
  105.9 2.7 %collective-permute-start.23 = (bf16[2,256,1024]{2,1,0:T(8,128)(2,1)S(1)}, bf16[2,256,1024]{2,1,0:T(8,128)(2,1)S(1)}, u32[]{:S(2)}, u32[]{:S(2)}) collective-permute-start(bf16[2,256,1024]{2,1,0:T(8,128)(2,1)S(1)} %bitcast.216), channel_id=1, source_target_pairs={{0,1},{1,0},{2,3},{3,2},{4,5},{5,4},{6,7},{7,6},{8,9},{9,8},{10,11... | collective-permute-start | bytes 3145736 | tf_op jit(solution)/shard_map/ppermute | solution.py:15
  106.7 3.4 %collective-permute-start.28 = (bf16[2,256,1024]{2,1,0:T(8,128)(2,1)S(1)}, bf16[2,256,1024]{2,1,0:T(8,128)(2,1)S(1)}, u32[]{:S(2)}, u32[]{:S(2)}) collective-permute-start(bf16[2,256,1024]{2,1,0:T(8,128)(2,1)S(1)} %bitcast.215), channel_id=1, source_target_pairs={{0,1},{1,0},{2,3},{3,2},{4,5},{5,4},{6,7},{7,6},{8,9},{9,8},{10,11... | collective-permute-start | bytes 3145736 | tf_op jit(solution)/shard_map/ppermute | solution.py:15
  107.5 30.5 %collective-permute-start.9 = (bf16[1,128,1024]{2,1,0:T(8,128)(2,1)S(1)}, bf16[1,128,1024]{2,1,0:T(8,128)(2,1)S(1)}, u32[]{:S(2)}, u32[]{:S(2)}) collective-permute-start(bf16[1,128,1024]{2,1,0:T(8,128)(2,1)S(1)} %fusion.34), channel_id=1, source_target_pairs={{0,8},{4,12},{8,0},{12,4},{1,9},{5,13},{9,1},{13,5},{2,10},{6,14},... | collective-permute-start | bytes 786440 | tf_op jit(solution)/shard_map/ppermute | solution.py:15
  109.5 15.3 %collective-permute-start.24 = (bf16[1,256,1024]{2,1,0:T(8,128)(2,1)S(1)}, bf16[1,256,1024]{2,1,0:T(8,128)(2,1)S(1)}, u32[]{:S(2)}, u32[]{:S(2)}) collective-permute-start(bf16[1,256,1024]{2,1,0:T(8,128)(2,1)S(1)} %fusion.24), channel_id=1, source_target_pairs={{0,2},{1,3},{2,0},{3,1},{4,6},{5,7},{6,4},{7,5},{8,10},{9,11},{10,... | collective-permute-start | bytes 1572872 | tf_op jit(solution)/shard_map/ppermute | solution.py:15
  115.2 6.3 %collective-permute-start.20 = (f32[128,64]{0,1:T(8,128)S(1)}, f32[128,64]{0,1:T(8,128)S(1)}, u32[]{:S(2)}, u32[]{:S(2)}) collective-permute-start(f32[128,64]{0,1:T(8,128)S(1)} %get-tuple-element.47), channel_id=1, source_target_pairs={{0,4},{4,0},{8,12},{12,8},{1,5},{5,1},{9,13},{13,9},{2,6},{6,2},{1... | collective-permute-start | bytes 98312 | tf_op jit(solution)/shard_map/ppermute | solution.py:15
  115.5 8.7 %collective-permute-start.21 = (f32[128,64]{0,1:T(8,128)S(1)}, f32[128,64]{0,1:T(8,128)S(1)}, u32[]{:S(2)}, u32[]{:S(2)}) collective-permute-start(f32[128,64]{0,1:T(8,128)S(1)} %get-tuple-element.49), channel_id=1, source_target_pairs={{0,8},{4,12},{8,0},{12,4},{1,9},{5,13},{9,1},{13,5},{2,10},{6,14},... | collective-permute-start | bytes 98312 | tf_op jit(solution)/shard_map/ppermute | solution.py:15
  117.4 6.8 %collective-permute-start.22 = (f32[128,64]{0,1:T(8,128)S(1)}, f32[128,64]{0,1:T(8,128)S(1)}, u32[]{:S(2)}, u32[]{:S(2)}) collective-permute-start(f32[128,64]{0,1:T(8,128)S(1)} %get-tuple-element.48), channel_id=1, source_target_pairs={{0,12},{4,8},{8,4},{12,0},{1,13},{5,9},{9,5},{13,1},{2,14},{6,10},... | collective-permute-start | bytes 98312 | tf_op jit(solution)/shard_map/ppermute | solution.py:15
  121.5 13.9 %collective-permute-start.29 = (bf16[1,256,1024]{2,1,0:T(8,128)(2,1)S(1)}, bf16[1,256,1024]{2,1,0:T(8,128)(2,1)S(1)}, u32[]{:S(2)}, u32[]{:S(2)}) collective-permute-start(bf16[1,256,1024]{2,1,0:T(8,128)(2,1)S(1)} %fusion.25), channel_id=1, source_target_pairs={{0,2},{1,3},{2,0},{3,1},{4,6},{5,7},{6,4},{7,5},{8,10},{9,11},{10,... | collective-permute-start | bytes 1572872 | tf_op jit(solution)/shard_map/ppermute | solution.py:15
  124.7 17.6 %collective-permute-start.33 = (bf16[2,256,1024]{2,1,0:T(8,128)(2,1)S(1)}, bf16[2,256,1024]{2,1,0:T(8,128)(2,1)S(1)}, u32[]{:S(2)}, u32[]{:S(2)}) collective-permute-start(bf16[2,256,1024]{2,1,0:T(8,128)(2,1)S(1)} %bitcast.196), channel_id=1, source_target_pairs={{0,1},{1,0},{2,3},{3,2},{4,5},{5,4},{6,7},{7,6},{8,9},{9,8},{10,11... | collective-permute-start | bytes 3145736 | tf_op jit(solution)/shard_map/ppermute | solution.py:15
  125.0 19.5 %collective-permute-start.26 = (bf16[64,1024]{1,0:T(8,128)(2,1)S(1)}, bf16[64,1024]{1,0:T(8,128)(2,1)S(1)}, u32[]{:S(2)}, u32[]{:S(2)}) collective-permute-start(bf16[64,1024]{1,0:T(8,128)(2,1)S(1)} %get-tuple-element.43), channel_id=1, source_target_pairs={{0,8},{4,12},{8,0},{12,4},{1,9},{5,13},{9,1},{13,5},{2,10},{6,14},... | collective-permute-start | bytes 393224 | tf_op jit(solution)/shard_map/ppermute | solution.py:15
  126.6 12.8 %collective-permute-start.25 = (bf16[64,1024]{1,0:T(8,128)(2,1)S(1)}, bf16[64,1024]{1,0:T(8,128)(2,1)S(1)}, u32[]{:S(2)}, u32[]{:S(2)}) collective-permute-start(bf16[64,1024]{1,0:T(8,128)(2,1)S(1)} %get-tuple-element.44), channel_id=1, source_target_pairs={{0,4},{4,0},{8,12},{12,8},{1,5},{5,1},{9,13},{13,9},{2,6},{6,2},{1... | collective-permute-start | bytes 393224 | tf_op jit(solution)/shard_map/ppermute | solution.py:15
  135.4 10.3 %collective-permute-start.27 = (bf16[64,1024]{1,0:T(8,128)(2,1)S(1)}, bf16[64,1024]{1,0:T(8,128)(2,1)S(1)}, u32[]{:S(2)}, u32[]{:S(2)}) collective-permute-start(bf16[64,1024]{1,0:T(8,128)(2,1)S(1)} %get-tuple-element.42), channel_id=1, source_target_pairs={{0,12},{4,8},{8,4},{12,0},{1,13},{5,9},{9,5},{13,1},{2,14},{6,10},... | collective-permute-start | bytes 393224 | tf_op jit(solution)/shard_map/ppermute | solution.py:15
  138.0 21.0 %collective-permute-start.30 = (bf16[64,1024]{1,0:T(8,128)(2,1)}, bf16[64,1024]{1,0:T(8,128)(2,1)S(1)}, u32[]{:S(2)}, u32[]{:S(2)}) collective-permute-start(bf16[64,1024]{1,0:T(8,128)(2,1)} %get-tuple-element.41), channel_id=1, source_target_pairs={{0,4},{4,0},{8,12},{12,8},{1,5},{5,1},{9,13},{13,9},{2,6},{6,2},{1... | collective-permute-start | bytes 393224 | tf_op jit(solution)/shard_map/ppermute | solution.py:15
  139.4 19.6 %collective-permute-start.31 = (bf16[64,1024]{1,0:T(8,128)(2,1)}, bf16[64,1024]{1,0:T(8,128)(2,1)}, u32[]{:S(2)}, u32[]{:S(2)}) collective-permute-start(bf16[64,1024]{1,0:T(8,128)(2,1)} %get-tuple-element.40), channel_id=1, source_target_pairs={{0,8},{4,12},{8,0},{12,4},{1,9},{5,13},{9,1},{13,5},{2,10},{6,14},... | collective-permute-start | bytes 393224 | tf_op jit(solution)/shard_map/ppermute | solution.py:15
  142.2 25.0 %collective-permute-start.32 = (bf16[64,1024]{1,0:T(8,128)(2,1)}, bf16[64,1024]{1,0:T(8,128)(2,1)}, u32[]{:S(2)}, u32[]{:S(2)}) collective-permute-start(bf16[64,1024]{1,0:T(8,128)(2,1)} %get-tuple-element.39), channel_id=1, source_target_pairs={{0,12},{4,8},{8,4},{12,0},{1,13},{5,9},{9,5},{13,1},{2,14},{6,10},... | collective-permute-start | bytes 393224 | tf_op jit(solution)/shard_map/ppermute | solution.py:15
  144.5 12.8 %copy-start.4 = (bf16[64,1024]{1,0:T(8,128)(2,1)}, bf16[64,1024]{1,0:T(8,128)(2,1)S(1)}, u32[]{:S(2)}) copy-start(bf16[64,1024]{1,0:T(8,128)(2,1)S(1)} %collective-permute-done.26.refs_0_) | copy-start | bytes 393220
  144.5 11.9 %collective-permute-start.34 = (bf16[1,256,1024]{2,1,0:T(8,128)(2,1)S(1)}, bf16[1,256,1024]{2,1,0:T(8,128)(2,1)S(1)}, u32[]{:S(2)}, u32[]{:S(2)}) collective-permute-start(bf16[1,256,1024]{2,1,0:T(8,128)(2,1)S(1)} %fusion.26), channel_id=1, source_target_pairs={{0,2},{1,3},{2,0},{3,1},{4,6},{5,7},{6,4},{7,5},{8,10},{9,11},{10,... | collective-permute-start | bytes 1572872 | tf_op jit(solution)/shard_map/ppermute | solution.py:15
  159.0 6.9 %collective-permute-start.35 = (bf16[2,64,1024]{2,1,0:T(8,128)(2,1)}, bf16[2,64,1024]{2,1,0:T(8,128)(2,1)S(1)}, u32[]{:S(2)}, u32[]{:S(2)}) collective-permute-start(bf16[2,64,1024]{2,1,0:T(8,128)(2,1)} %bitcast.208), channel_id=1, source_target_pairs={{0,4},{4,0},{8,12},{12,8},{1,5},{5,1},{9,13},{13,9},{2,6},{6,2},{1... | collective-permute-start | bytes 786440 | tf_op jit(solution)/shard_map/ppermute | solution.py:15
  166.0 6.6 %collective-permute-start.36 = (bf16[1,64,1024]{2,1,0:T(8,128)(2,1)S(1)}, bf16[1,64,1024]{2,1,0:T(8,128)(2,1)S(1)}, u32[]{:S(2)}, u32[]{:S(2)}) collective-permute-start(bf16[1,64,1024]{2,1,0:T(8,128)(2,1)S(1)} %fusion.42), channel_id=1, source_target_pairs={{0,8},{4,12},{8,0},{12,4},{1,9},{5,13},{9,1},{13,5},{2,10},{6,14},... | collective-permute-start | bytes 393224 | tf_op jit(solution)/shard_map/ppermute | solution.py:15
  168.2 5.1 %copy-start.1 = (f32[64,8192]{1,0:T(8,128)}, f32[64,8192]{1,0:T(8,128)S(1)}, u32[]{:S(2)}) copy-start(f32[64,8192]{1,0:T(8,128)S(1)} %convert_dynamic-update-slice_fusion) | copy-start | bytes 6291460

commit v3 on v2

--- a/solution.py
+++ b/solution.py
@@ -156,12 +156,18 @@
 
     up_first = swap(up[None], "fsdp", n_f // 2)
     up_own, _, _ = gather(up, "fsdp", up_first)
-    up_all, up_across, up_last = gather(up_own, "rows")
+    up_all, _, _ = gather(up_own, "rows")
     up_all = up_all.reshape(owners * rank, outputs)
     down_pieces = exchange(cut(down_t, depth, 0, up_first), "fsdp")
     down_own = jnp.stack(down_pieces)
-    down_all, _, _ = gather(down_own, "rows")
-    down_all = down_all.reshape(owners * rank, depth)
+    held, bit = down_own[None], n_r // 2
+    while bit > 1:
+        got = swap(held, "rows", bit)
+        held = jnp.stack([held, got], 1).reshape((-1,) + down_own.shape)
+        bit //= 2
+    downs = [
+        h.reshape(owners // 2 * rank, depth) for h in (held, swap(held, "rows", 1))
+    ]
 
     back = (adapter_scale * pick(dot(output_gradient, up_all, 1, 1), ids, all_ids)).astype(bf16)
     packed = jnp.concatenate(
@@ -173,21 +179,21 @@
     back_even = spread(back_rows, row_ids, even_ids)
     back_odd = spread(back_rows, row_ids, odd_ids)
 
-    group = owners
-    while group * rank * row_ids.shape[0] > 1 << 21 and group % 2 == 0:
+    group = owners // 2
+    while group * rank * row_ids.shape[0] > 1 << 20 and group % 2 == 0:
         group //= 2
 
-    def hidden_of(x_part, down_part):
-        if group == owners:
-            return pick(dot(x_part, down_part, 1, 1), row_ids, all_ids)
+    def hidden_of(x_part, down_part, names):
+        if group == owners // 2:
+            return pick(dot(x_part, down_part, 1, 1), row_ids, names)
 
         def one(g, total):
             down = lax.dynamic_slice_in_dim(down_part, g * group * rank, group * rank, 0)
-            names = lax.dynamic_slice_in_dim(all_ids, g * group, group, 0)
-            return total + pick(dot(x_part, down, 1, 1), row_ids, names)
+            some = lax.dynamic_slice_in_dim(names, g * group, group, 0)
+            return total + pick(dot(x_part, down, 1, 1), row_ids, some)
 
         return lax.fori_loop(
-            0, owners // group, one, jnp.zeros((row_ids.shape[0], rank), f32)
+            0, owners // 2 // group, one, jnp.zeros((row_ids.shape[0], rank), f32)
         )
 
     base = 0.0
@@ -204,7 +210,8 @@
         grad_pieces.append(scatter(even, odd, "rows"))
         span = slice(c * part, (c + 1) * part)
         base = base + dot(x_part, frozen_key_weight[span], 1, 0)
-        hidden_part = hidden_part + hidden_of(x_part, down_all[:, span])
+        for d, h in zip(downs, (even_ids, odd_ids)):
+            hidden_part = hidden_part + hidden_of(x_part, d[:, span], h)
 
     hidden = exchange(list(hidden_part.reshape(n_f, count, rank)), "fsdp")
     hidden = sum(hidden[1:], hidden[0]).astype(bf16)
@@ -232,7 +239,7 @@
             got = down_moved[c][n].astype(f32)
             grad_down = lax.dynamic_update_slice_in_dim(grad_down, got, at, 1)
     pairs = up_grad.reshape(n_f // 2, 2, rank, outputs)
-    odd = copied(pairs[:, 1].astype(bf16), down_moved[0][n_f // 2])
+    odd = copied(pairs[:, 1].astype(bf16), down_moved[0][1])
     up_grad = scatter(pairs[:, 0], odd, "fsdp")
 
     return (mixed, jnp.swapaxes(grad_down, 0, 1)[None], up_grad[None])

time: 174 us -> 173 us (level)
    another operation x7 -> x4, other arithmetic: 6.59 us -> 2.58 us  [gather(): held = jnp.stack([held, got], 1).reshape((-1,) + a.shape)]
    another operation x2 -> x4, other arithmetic: 0.41 us -> 4 us  [the longest x2 3.63 us: per_device(): held = jnp.stack([held, got], 1).reshape((-1,) + down_own.shape)]
    dot_general x12 -> x14, matrix products: 10.8 us -> 11.1 us  [dot(): lax.dot_general(a, b, (((da,), (db,)), ((), ())), preferred_element_type=...]
where the time goes in v3:
time: 173 us
  waiting for transfers between devices  84 us (49%)
  starting transfers between devices  47.8 us (28%)
  other arithmetic  12.9 us (7%)
  matrix products  11.1 us (6%)
  local copies, waits for them, and re-layouts  7.88 us (5%)
  Pallas kernels  7.64 us (4%)
    ppermute x37, waiting for transfers between devices, swap(): return lax.ppermute(a, axis, [(i, i ^ bits) for i in range(n)])  84 us
    ppermute x37, starting transfers between devices, swap(): return lax.ppermute(a, axis, [(i, i ^ bits) for i in range(n)])  47.8 us
    dot_general x14, matrix products, dot(): lax.dot_general(a, b, (((da,), (db,)), ((), ())), preferred_element_type=...  11.1 us
    pallas_call x3, Pallas kernels, cut(): pl.pallas_call(body, out_shape=[jax.ShapeDtypeStruct((a.shape[0], size),...  5.97 us
    unnamed x24, local copies, waits for them, and re-layouts  4.1 us
    another operation x2, other arithmetic, per_device(): held = jnp.stack([held, got], 1).reshape((-1,) + down_own.shape)  3.63 us
  transfers between devices with their start and end apart: 37, of which 15 were waited for; matrix products, arithmetic and copies ran while one was open for 17% of the time, Pallas kernels for 3%

profile of v3, /device:TPU:0, one launch (start us, length us, event | category | flops | bytes accessed | tf_op | source)
XLA Modules:
  0.0 172.8 jit_solution(7918514658935390276)
XLA Ops:
  0.6 4.1 %collective-permute-start = (bf16[1,64,1024]{2,1,0:T(8,128)(2,1)}, bf16[1,64,1024]{2,1,0:T(8,128)(2,1)S(1)}, u32[]{:S(2)}, u32[]{:S(2)}) collective-permute-start(bf16[1,64,1024]{2,1,0:T(8,128)(2,1)} %param.10), channel_id=1, source_target_pairs={{0,8},{4,12},{8,0},{12,4},{1,9},{5,13},{9,1},{13,5},{2,10},{6,14},... | collective-permute-start | bytes 393224 | tf_op jit(solution)/shard_map/ppermute | solution.py:15
  5.1 0.7 broadcast_compare_fusion.3
  5.9 0.7 broadcast_compare_fusion.2
  6.6 4.7 %collective-permute-done.refs_0_ = bf16[1,64,1024]{2,1,0:T(8,128)(2,1)S(1)} collective-permute-done((bf16[1,64,1024]{2,1,0:T(8,128)(2,1)}, bf16[1,64,1024]{2,1,0:T(8,128)(2,1)S(1)}, u32[]{:S(2)}, u32[]{:S(2)}) %collective-permute-start) | collective-permute-done | bytes 131104 | tf_op jit(solution)/shard_map/ppermute | solution.py:15
  11.9 2.0 %shard_map.88 = (bf16[64,2048]{1,0:T(8,128)(2,1)}, bf16[64,2048]{1,0:T(8,128)(2,1)}, bf16[64,2048]{1,0:T(8,128)(2,1)}, bf16[64,2048]{1,0:T(8,128)(2,1)}) custom-call(s32[1]{0:T(128)} %bitcast.index, bf16[64,8192]{1,0:T(8,128)(2,1)} %bitcast.194, bf16[1,64,1024]{2,1,0:T(8,128)(2,1)} %copy-done.5), custom_call_target="tpu_custom_call" | custom-call | bytes 2097152 | tf_op jit(solution)/shard_map/pallas_call | solution.py:75
  14.0 4.1 %collective-permute-start.16 = (bf16[64,2048]{1,0:T(8,128)(2,1)}, bf16[64,2048]{1,0:T(8,128)(2,1)S(1)}, u32[]{:S(2)}, u32[]{:S(2)}) collective-permute-start(bf16[64,2048]{1,0:T(8,128)(2,1)} %get-tuple-element.25), channel_id=1, source_target_pairs={{0,4},{4,0},{8,12},{12,8},{1,5},{5,1},{9,13},{13,9},{2,6},{6,2},{1... | collective-permute-start | bytes 786440 | tf_op jit(solution)/shard_map/ppermute | solution.py:15
  18.4 1.0 fusion.43
  19.8 0.7 convert_bitcast_fusion
  20.4 14.6 %collective-permute-done.1.refs_0_ = bf16[64,2048]{1,0:T(8,128)(2,1)S(1)} collective-permute-done((bf16[64,2048]{1,0:T(8,128)(2,1)}, bf16[64,2048]{1,0:T(8,128)(2,1)S(1)}, u32[]{:S(2)}, u32[]{:S(2)}) %collective-permute-start.1) | collective-permute-done | bytes 262176 | tf_op jit(solution)/shard_map/ppermute | solution.py:15
  35.1 0.7 copy-done.2
  35.8 2.0 %shard_map.89 = (bf16[128,1024]{1,0:T(8,128)(2,1)}, bf16[128,1024]{1,0:T(8,128)(2,1)}, bf16[128,1024]{1,0:T(8,128)(2,1)}, bf16[128,1024]{1,0:T(8,128)(2,1)}) custom-call(s32[1]{0:T(128)} %bitcast.index, bf16[128,8192]{1,0:T(8,128)(2,1)} %source.3, bf16[64,2048]{1,0:T(8,128)(2,1)} %copy-done.2), custom_call_target="tpu_custom_call" | custom-call | bytes 2097152 | tf_op jit(solution)/shard_map/pallas_call | solution.py:75
  37.9 2.1 %fusion.41 = (bf16[1,1,4,64,2048]{4,3,2,1,0:T(8,128)(2,1)S(1)}, bf16[1,4,64,2048]{3,2,1,0:T(8,128)(2,1)}) fusion(bf16[1,64,2048]{2,1,0:T(8,128)(2,1)S(1)} %bitcast.210, bf16[1,64,2048]{2,1,0:T(8,128)(2,1)} %bitcast.193, bf16[1,64,2048]{2,1,0:T(8,128)(2,1)S(1)} %bitcast.209, bf16[1,64,2048]{2,1,0:T(8,128)(2,1)S(1)} %bitcast.208), kind=kLoop, calls=%fused_computation.83 | loop fusion | flops 1572864 | bytes 3145728 | tf_op jit(solution)/shard_map/stack;broadcast_in_dim | solution.py:166
  40.1 1.6 collective-permute-start.18
  41.6 8.9 %collective-permute-start.2 = (bf16[128,1024]{1,0:T(8,128)(2,1)}, bf16[128,1024]{1,0:T(8,128)(2,1)S(1)}, u32[]{:S(2)}, u32[]{:S(2)}) collective-permute-start(bf16[128,1024]{1,0:T(8,128)(2,1)} %get-tuple-element.17), channel_id=1, source_target_pairs={{0,4},{4,0},{8,12},{12,8},{1,5},{5,1},{9,13},{13,9},{2,6},{6,2},{1... | collective-permute-start | bytes 786440 | tf_op jit(solution)/shard_map/ppermute | solution.py:15
  50.8 4.6 %collective-permute-done.3.refs_0_ = bf16[128,1024]{1,0:T(8,128)(2,1)S(1)} collective-permute-done((bf16[128,1024]{1,0:T(8,128)(2,1)}, bf16[128,1024]{1,0:T(8,128)(2,1)S(1)}, u32[]{:S(2)}, u32[]{:S(2)}) %collective-permute-start.3) | collective-permute-done | bytes 262176 | tf_op jit(solution)/shard_map/ppermute | solution.py:15
  55.4 0.7 copy-done.3
  56.1 2.0 %shard_map.90 = (bf16[128,1024]{1,0:T(8,128)(2,1)}, bf16[128,1024]{1,0:T(8,128)(2,1)}, bf16[128,1024]{1,0:T(8,128)(2,1)}, bf16[128,1024]{1,0:T(8,128)(2,1)}) custom-call(s32[1]{0:T(128)} %bitcast.index, bf16[128,8192]{1,0:T(8,128)(2,1)} %source.3, bf16[128,1024]{1,0:T(8,128)(2,1)} %copy-done.3), custom_call_target="tpu_custom_call" | custom-call | bytes 2097152 | tf_op jit(solution)/shard_map/pallas_call | solution.py:75
  58.1 1.0 constant_dynamic-update-slice_fusion.7
  59.2 2.6 %collective-permute-done.2 = bf16[128,1024]{1,0:T(8,128)(2,1)S(1)} collective-permute-done((bf16[128,1024]{1,0:T(8,128)(2,1)}, bf16[128,1024]{1,0:T(8,128)(2,1)S(1)}, u32[]{:S(2)}, u32[]{:S(2)}) %collective-permute-start.2) | collective-permute-done | bytes 262176 | tf_op jit(solution)/shard_map/ppermute | solution.py:15
  61.8 1.0 constant_dynamic-update-slice_fusion.1
  62.8 2.2 %collective-permute-start.7 = (bf16[128,1024]{1,0:T(8,128)(2,1)}, bf16[128,1024]{1,0:T(8,128)(2,1)S(1)}, u32[]{:S(2)}, u32[]{:S(2)}) collective-permute-start(bf16[128,1024]{1,0:T(8,128)(2,1)} %get-tuple-element.23), channel_id=1, source_target_pairs={{0,12},{4,8},{8,4},{12,0},{1,13},{5,9},{9,5},{13,1},{2,14},{6,10},... | collective-permute-start | bytes 786440 | tf_op jit(solution)/shard_map/ppermute | solution.py:15
  65.0 1.0 constant_dynamic-update-slice_fusion
  66.0 7.8 %collective-permute-done.11 = bf16[1,4,64,1024]{3,2,1,0:T(8,128)(2,1)} collective-permute-done((bf16[1,4,64,1024]{3,2,1,0:T(8,128)(2,1)S(1)}, bf16[1,4,64,1024]{3,2,1,0:T(8,128)(2,1)}, u32[]{:S(2)}, u32[]{:S(2)}) %collective-permute-start.11) | collective-permute-done | bytes 524320 | tf_op jit(solution)/shard_map/ppermute | solution.py:15
  73.8 1.3 fusion.25
  75.2 6.8 %collective-permute-done.6 = bf16[128,1024]{1,0:T(8,128)(2,1)S(1)} collective-permute-done((bf16[128,1024]{1,0:T(8,128)(2,1)}, bf16[128,1024]{1,0:T(8,128)(2,1)S(1)}, u32[]{:S(2)}, u32[]{:S(2)}) %collective-permute-start.6) | collective-permute-done | bytes 262176 | tf_op jit(solution)/shard_map/ppermute | solution.py:15
  82.1 1.3 fusion
  83.4 1.3 fusion.4
  84.7 3.7 %collective-permute-start.8 = (bf16[2,128,1024]{2,1,0:T(8,128)(2,1)S(1)}, bf16[2,128,1024]{2,1,0:T(8,128)(2,1)S(1)}, u32[]{:S(2)}, u32[]{:S(2)}) collective-permute-start(bf16[2,128,1024]{2,1,0:T(8,128)(2,1)S(1)} %fusion.29), channel_id=1, source_target_pairs={{0,4},{4,0},{8,12},{12,8},{1,5},{5,1},{9,13},{13,9},{2,6},{6,2},{1... | collective-permute-start | bytes 1572872 | tf_op jit(solution)/shard_map/ppermute | solution.py:15
  88.4 1.5 pad_maximum_fusion.1
  90.4 0.7 fusion.54
  91.2 3.8 %collective-permute-start.14 = (bf16[128,128]{0,1:T(8,128)(2,1)S(1)}, bf16[128,128]{0,1:T(8,128)(2,1)S(1)}, u32[]{:S(2)}, u32[]{:S(2)}) collective-permute-start(bf16[128,128]{0,1:T(8,128)(2,1)S(1)} %pad_maximum_fusion.10), channel_id=1, source_target_pairs={{0,8},{4,12},{8,0},{12,4},{1,9},{5,13},{9,1},{13,5},{2,10},{6,14},... | collective-permute-start | bytes 98312 | tf_op jit(solution)/shard_map/ppermute | solution.py:15
  95.6 0.7 fusion.16
  96.4 4.9 %collective-permute-done.13 = bf16[128,128]{0,1:T(8,128)(2,1)S(1)} collective-permute-done((bf16[128,128]{0,1:T(8,128)(2,1)S(1)}, bf16[128,128]{0,1:T(8,128)(2,1)S(1)}, u32[]{:S(2)}, u32[]{:S(2)}) %collective-permute-start.13) | collective-permute-done | bytes 32800 | tf_op jit(solution)/shard_map/ppermute | solution.py:15
  101.4 3.7 %collective-permute-done.15 = bf16[128,128]{0,1:T(8,128)(2,1)S(1)} collective-permute-done((bf16[128,128]{0,1:T(8,128)(2,1)S(1)}, bf16[128,128]{0,1:T(8,128)(2,1)S(1)}, u32[]{:S(2)}, u32[]{:S(2)}) %collective-permute-start.15) | collective-permute-done | bytes 32800 | tf_op jit(solution)/shard_map/ppermute | solution.py:15
  105.2 0.7 convolution_convert_fusion.1
  106.0 0.7 fusion.20
  106.8 0.7 convolution_convert_fusion
  108.7 0.7 add_bitcast_fusion.2
  110.4 0.7 add_bitcast_fusion.1
  111.1 0.7 fusion.14
  111.8 0.7 fusion.18
  112.9 0.9 collective-permute-start.20
  113.8 2.0 %collective-permute-start.21 = (f32[128,64]{0,1:T(8,128)S(1)}, f32[128,64]{0,1:T(8,128)S(1)}, u32[]{:S(2)}, u32[]{:S(2)}) collective-permute-start(f32[128,64]{0,1:T(8,128)S(1)} %get-tuple-element.51), channel_id=1, source_target_pairs={{0,8},{4,12},{8,0},{12,4},{1,9},{5,13},{9,1},{13,5},{2,10},{6,14},... | collective-permute-start | bytes 98312 | tf_op jit(solution)/shard_map/ppermute | solution.py:15
  115.8 1.6 collective-permute-start.22
  117.7 1.7 %collective-permute-start.29 = (bf16[1,256,1024]{2,1,0:T(8,128)(2,1)S(1)}, bf16[1,256,1024]{2,1,0:T(8,128)(2,1)S(1)}, u32[]{:S(2)}, u32[]{:S(2)}) collective-permute-start(bf16[1,256,1024]{2,1,0:T(8,128)(2,1)S(1)} %fusion.27), channel_id=1, source_target_pairs={{0,2},{1,3},{2,0},{3,1},{4,6},{5,7},{6,4},{7,5},{8,10},{9,11},{10,... | collective-permute-start | bytes 1572872 | tf_op jit(solution)/shard_map/ppermute | solution.py:15
  119.4 5.6 %collective-permute-done.21 = f32[128,64]{0,1:T(8,128)S(1)} collective-permute-done((f32[128,64]{0,1:T(8,128)S(1)}, f32[128,64]{0,1:T(8,128)S(1)}, u32[]{:S(2)}, u32[]{:S(2)}) %collective-permute-start.21) | collective-permute-done | bytes 32800 | tf_op jit(solution)/shard_map/ppermute | solution.py:15
  125.7 1.2 collective-permute-start.25
  127.0 0.8 collective-permute-start.26
  128.2 6.5 %collective-permute-done.29 = bf16[1,256,1024]{2,1,0:T(8,128)(2,1)S(1)} collective-permute-done((bf16[1,256,1024]{2,1,0:T(8,128)(2,1)S(1)}, bf16[1,256,1024]{2,1,0:T(8,128)(2,1)S(1)}, u32[]{:S(2)}, u32[]{:S(2)}) %collective-permute-start.29) | collective-permute-done | bytes 524320 | tf_op jit(solution)/shard_map/ppermute | solution.py:15
  134.8 2.1 %collective-permute-start.27 = (bf16[64,1024]{1,0:T(8,128)(2,1)S(1)}, bf16[64,1024]{1,0:T(8,128)(2,1)S(1)}, u32[]{:S(2)}, u32[]{:S(2)}) collective-permute-start(bf16[64,1024]{1,0:T(8,128)(2,1)S(1)} %get-tuple-element.44), channel_id=1, source_target_pairs={{0,12},{4,8},{8,4},{12,0},{1,13},{5,9},{9,5},{13,1},{2,14},{6,10},... | collective-permute-start | bytes 393224 | tf_op jit(solution)/shard_map/ppermute | solution.py:15
  137.1 0.8 slice_bitcast_fusion.8
  137.8 0.9 collective-permute-start.30
  138.7 1.2 fusion.35
  140.1 1.4 collective-permute-start.31
  141.6 2.2 %collective-permute-start.32 = (bf16[64,1024]{1,0:T(8,128)(2,1)}, bf16[64,1024]{1,0:T(8,128)(2,1)}, u32[]{:S(2)}, u32[]{:S(2)}) collective-permute-start(bf16[64,1024]{1,0:T(8,128)(2,1)} %get-tuple-element.41), channel_id=1, source_target_pairs={{0,12},{4,8},{8,4},{12,0},{1,13},{5,9},{9,5},{13,1},{2,14},{6,10},... | collective-permute-start | bytes 393224 | tf_op jit(solution)/shard_map/ppermute | solution.py:15
  144.9 10.9 %collective-permute-done.34 = bf16[1,256,1024]{2,1,0:T(8,128)(2,1)S(1)} collective-permute-done((bf16[1,256,1024]{2,1,0:T(8,128)(2,1)S(1)}, bf16[1,256,1024]{2,1,0:T(8,128)(2,1)S(1)}, u32[]{:S(2)}, u32[]{:S(2)}) %collective-permute-start.34) | collective-permute-done | bytes 524320 | tf_op jit(solution)/shard_map/ppermute | solution.py:15
  155.9 0.7 slice.247
  156.7 1.7 shard_map.91
  158.4 0.9 convert_dynamic-update-slice_fusion.1
  159.3 6.3 %collective-permute-done.35 = bf16[2,64,1024]{2,1,0:T(8,128)(2,1)S(1)} collective-permute-done((bf16[2,64,1024]{2,1,0:T(8,128)(2,1)}, bf16[2,64,1024]{2,1,0:T(8,128)(2,1)S(1)}, u32[]{:S(2)}, u32[]{:S(2)}) %collective-permute-start.35) | collective-permute-done | bytes 262176 | tf_op jit(solution)/shard_map/ppermute | solution.py:15
  165.7 0.8 collective-permute-start.36
  166.6 0.9 convert_dynamic-update-slice_fusion
  167.5 4.5 %collective-permute-done.36 = bf16[1,64,1024]{2,1,0:T(8,128)(2,1)S(1)} collective-permute-done((bf16[1,64,1024]{2,1,0:T(8,128)(2,1)S(1)}, bf16[1,64,1024]{2,1,0:T(8,128)(2,1)S(1)}, u32[]{:S(2)}, u32[]{:S(2)}) %collective-permute-start.36) | collective-permute-done | bytes 131104 | tf_op jit(solution)/shard_map/ppermute | solution.py:15
  172.0 0.7 fusion.37
  (112 shorter events, 9.4 us)
Async XLA Ops:
  0.6 89.7 %copy-start = (bf16[128,1024]{1,0:T(8,128)(2,1)S(1)}, bf16[128,1024]{1,0:T(8,128)(2,1)}, u32[]{:S(2)}) copy-start(bf16[128,1024]{1,0:T(8,128)(2,1)} %param.11) | copy-start | bytes 786436
  0.6 10.6 %collective-permute-start = (bf16[1,64,1024]{2,1,0:T(8,128)(2,1)}, bf16[1,64,1024]{2,1,0:T(8,128)(2,1)S(1)}, u32[]{:S(2)}, u32[]{:S(2)}) collective-permute-start(bf16[1,64,1024]{2,1,0:T(8,128)(2,1)} %param.10), channel_id=1, source_target_pairs={{0,8},{4,12},{8,0},{12,4},{1,9},{5,13},{9,1},{13,5},{2,10},{6,14},... | collective-permute-start | bytes 393224 | tf_op jit(solution)/shard_map/ppermute | solution.py:15
  11.3 0.7 copy-start.5
  13.9 24.0 %copy-start.6 = (bf16[64,2048]{1,0:T(8,128)(2,1)S(1)}, bf16[64,2048]{1,0:T(8,128)(2,1)}, u32[]{:S(2)}) copy-start(bf16[64,2048]{1,0:T(8,128)(2,1)} %get-tuple-element.24) | copy-start | bytes 786436
  13.9 21.2 %collective-permute-start.1 = (bf16[64,2048]{1,0:T(8,128)(2,1)}, bf16[64,2048]{1,0:T(8,128)(2,1)S(1)}, u32[]{:S(2)}, u32[]{:S(2)}) collective-permute-start(bf16[64,2048]{1,0:T(8,128)(2,1)} %get-tuple-element.15), channel_id=1, source_target_pairs={{0,8},{4,12},{8,0},{12,4},{1,9},{5,13},{9,1},{13,5},{2,10},{6,14},... | collective-permute-start | bytes 786440 | tf_op jit(solution)/shard_map/ppermute | solution.py:15
  14.0 23.9 %collective-permute-start.16 = (bf16[64,2048]{1,0:T(8,128)(2,1)}, bf16[64,2048]{1,0:T(8,128)(2,1)S(1)}, u32[]{:S(2)}, u32[]{:S(2)}) collective-permute-start(bf16[64,2048]{1,0:T(8,128)(2,1)} %get-tuple-element.25), channel_id=1, source_target_pairs={{0,4},{4,0},{8,12},{12,8},{1,5},{5,1},{9,13},{13,9},{2,6},{6,2},{1... | collective-permute-start | bytes 786440 | tf_op jit(solution)/shard_map/ppermute | solution.py:15
  18.1 19.8 %collective-permute-start.17 = (bf16[64,2048]{1,0:T(8,128)(2,1)}, bf16[64,2048]{1,0:T(8,128)(2,1)S(1)}, u32[]{:S(2)}, u32[]{:S(2)}) collective-permute-start(bf16[64,2048]{1,0:T(8,128)(2,1)} %get-tuple-element.26), channel_id=1, source_target_pairs={{0,12},{4,8},{8,4},{12,0},{1,13},{5,9},{9,5},{13,1},{2,14},{6,10},... | collective-permute-start | bytes 786440 | tf_op jit(solution)/shard_map/ppermute | solution.py:15
  19.4 31.2 %collective-permute-start.10 = (bf16[2,64,1024]{2,1,0:T(8,128)(2,1)S(1)}, bf16[2,64,1024]{2,1,0:T(8,128)(2,1)S(1)}, u32[]{:S(2)}, u32[]{:S(2)}) collective-permute-start(bf16[2,64,1024]{2,1,0:T(8,128)(2,1)S(1)} %get-tuple-element.48), channel_id=1, source_target_pairs={{0,4},{4,0},{8,12},{12,8},{1,5},{5,1},{9,13},{13,9},{2,6},{6,2},{1... | collective-permute-start | bytes 786440 | tf_op jit(solution)/shard_map/ppermute | solution.py:15
  35.1 0.7 copy-start.2
  37.8 17.6 %collective-permute-start.3 = (bf16[128,1024]{1,0:T(8,128)(2,1)}, bf16[128,1024]{1,0:T(8,128)(2,1)S(1)}, u32[]{:S(2)}, u32[]{:S(2)}) collective-permute-start(bf16[128,1024]{1,0:T(8,128)(2,1)} %get-tuple-element.18), channel_id=1, source_target_pairs={{0,8},{4,12},{8,0},{12,4},{1,9},{5,13},{9,1},{13,5},{2,10},{6,14},... | collective-permute-start | bytes 786440 | tf_op jit(solution)/shard_map/ppermute | solution.py:15
  37.9 12.8 %copy-start.7 = (bf16[128,1024]{1,0:T(8,128)(2,1)S(1)}, bf16[128,1024]{1,0:T(8,128)(2,1)}, u32[]{:S(2)}) copy-start(bf16[128,1024]{1,0:T(8,128)(2,1)} %get-tuple-element.16) | copy-start | bytes 786436
  40.1 48.3 %collective-permute-start.18 = (bf16[1,4,64,2048]{3,2,1,0:T(8,128)(2,1)}, bf16[1,4,64,2048]{3,2,1,0:T(8,128)(2,1)}, u32[]{:S(2)}, u32[]{:S(2)}) collective-permute-start(bf16[1,4,64,2048]{3,2,1,0:T(8,128)(2,1)} %get-tuple-element.40), channel_id=1, source_target_pairs={{0,2},{1,3},{2,0},{3,1},{4,6},{5,7},{6,4},{7,5},{8,10},{9,11},{10,... | collective-permute-start | bytes 3145736 | tf_op jit(solution)/shard_map/ppermute | solution.py:15
  41.6 20.2 %collective-permute-start.2 = (bf16[128,1024]{1,0:T(8,128)(2,1)}, bf16[128,1024]{1,0:T(8,128)(2,1)S(1)}, u32[]{:S(2)}, u32[]{:S(2)}) collective-permute-start(bf16[128,1024]{1,0:T(8,128)(2,1)} %get-tuple-element.17), channel_id=1, source_target_pairs={{0,4},{4,0},{8,12},{12,8},{1,5},{5,1},{9,13},{13,9},{2,6},{6,2},{1... | collective-permute-start | bytes 786440 | tf_op jit(solution)/shard_map/ppermute | solution.py:15
  50.6 23.2 %collective-permute-start.11 = (bf16[1,4,64,1024]{3,2,1,0:T(8,128)(2,1)S(1)}, bf16[1,4,64,1024]{3,2,1,0:T(8,128)(2,1)}, u32[]{:S(2)}, u32[]{:S(2)}) collective-permute-start(bf16[1,4,64,1024]{3,2,1,0:T(8,128)(2,1)S(1)} %bitcast.188), channel_id=1, source_target_pairs={{0,2},{1,3},{2,0},{3,1},{4,6},{5,7},{6,4},{7,5},{8,10},{9,11},{10,... | collective-permute-start | bytes 1572872 | tf_op jit(solution)/shard_map/ppermute | solution.py:15
  50.7 12.0 %collective-permute-start.4 = (bf16[128,1024]{1,0:T(8,128)(2,1)}, bf16[128,1024]{1,0:T(8,128)(2,1)}, u32[]{:S(2)}, u32[]{:S(2)}) collective-permute-start(bf16[128,1024]{1,0:T(8,128)(2,1)} %get-tuple-element.19), channel_id=1, source_target_pairs={{0,12},{4,8},{8,4},{12,0},{1,13},{5,9},{9,5},{13,1},{2,14},{6,10},... | collective-permute-start | bytes 786440 | tf_op jit(solution)/shard_map/ppermute | solution.py:15
  55.4 0.7 copy-start.3
  59.1 16.1 %collective-permute-start.5 = (bf16[128,1024]{1,0:T(8,128)(2,1)}, bf16[128,1024]{1,0:T(8,128)(2,1)S(1)}, u32[]{:S(2)}, u32[]{:S(2)}) collective-permute-start(bf16[128,1024]{1,0:T(8,128)(2,1)} %get-tuple-element.21), channel_id=1, source_target_pairs={{0,4},{4,0},{8,12},{12,8},{1,5},{5,1},{9,13},{13,9},{2,6},{6,2},{1... | collective-permute-start | bytes 786440 | tf_op jit(solution)/shard_map/ppermute | solution.py:15
  61.8 20.3 %collective-permute-start.6 = (bf16[128,1024]{1,0:T(8,128)(2,1)}, bf16[128,1024]{1,0:T(8,128)(2,1)S(1)}, u32[]{:S(2)}, u32[]{:S(2)}) collective-permute-start(bf16[128,1024]{1,0:T(8,128)(2,1)} %get-tuple-element.22), channel_id=1, source_target_pairs={{0,8},{4,12},{8,0},{12,4},{1,9},{5,13},{9,1},{13,5},{2,10},{6,14},... | collective-permute-start | bytes 786440 | tf_op jit(solution)/shard_map/ppermute | solution.py:15
  62.8 19.3 %collective-permute-start.7 = (bf16[128,1024]{1,0:T(8,128)(2,1)}, bf16[128,1024]{1,0:T(8,128)(2,1)S(1)}, u32[]{:S(2)}, u32[]{:S(2)}) collective-permute-start(bf16[128,1024]{1,0:T(8,128)(2,1)} %get-tuple-element.23), channel_id=1, source_target_pairs={{0,12},{4,8},{8,4},{12,0},{1,13},{5,9},{9,5},{13,1},{2,14},{6,10},... | collective-permute-start | bytes 786440 | tf_op jit(solution)/shard_map/ppermute | solution.py:15
  73.8 8.3 %copy-start.8 = (bf16[2048,1024]{1,0:T(8,128)(2,1)S(1)}, bf16[2048,1024]{1,0:T(8,128)(2,1)}, u32[]{:S(2)}) copy-start(bf16[2048,1024]{1,0:T(8,128)(2,1)} %param.8) | copy-start | bytes 12582916
  75.1 14.8 %collective-permute-start.12 = (bf16[2,4,64,1024]{3,2,1,0:T(8,128)(2,1)S(1)}, bf16[2,4,64,1024]{3,2,1,0:T(8,128)(2,1)S(1)}, u32[]{:S(2)}, u32[]{:S(2)}) collective-permute-start(bf16[2,4,64,1024]{3,2,1,0:T(8,128)(2,1)S(1)} %get-tuple-element.38), channel_id=1, source_target_pairs={{0,1},{1,0},{2,3},{3,2},{4,5},{5,4},{6,7},{7,6},{8,9},{9,8},{10,11... | collective-permute-start | bytes 3145736 | tf_op jit(solution)/shard_map/ppermute | solution.py:15
  84.7 23.3 %collective-permute-start.8 = (bf16[2,128,1024]{2,1,0:T(8,128)(2,1)S(1)}, bf16[2,128,1024]{2,1,0:T(8,128)(2,1)S(1)}, u32[]{:S(2)}, u32[]{:S(2)}) collective-permute-start(bf16[2,128,1024]{2,1,0:T(8,128)(2,1)S(1)} %fusion.29), channel_id=1, source_target_pairs={{0,4},{4,0},{8,12},{12,8},{1,5},{5,1},{9,13},{13,9},{2,6},{6,2},{1... | collective-permute-start | bytes 1572872 | tf_op jit(solution)/shard_map/ppermute | solution.py:15
  91.2 10.2 %collective-permute-start.13 = (bf16[128,128]{0,1:T(8,128)(2,1)S(1)}, bf16[128,128]{0,1:T(8,128)(2,1)S(1)}, u32[]{:S(2)}, u32[]{:S(2)}) collective-permute-start(bf16[128,128]{0,1:T(8,128)(2,1)S(1)} %pad_maximum_fusion.10), channel_id=1, source_target_pairs={{0,4},{4,0},{8,12},{12,8},{1,5},{5,1},{9,13},{13,9},{2,6},{6,2},{1... | collective-permute-start | bytes 98312 | tf_op jit(solution)/shard_map/ppermute | solution.py:15
  91.2 10.1 %collective-permute-start.14 = (bf16[128,128]{0,1:T(8,128)(2,1)S(1)}, bf16[128,128]{0,1:T(8,128)(2,1)S(1)}, u32[]{:S(2)}, u32[]{:S(2)}) collective-permute-start(bf16[128,128]{0,1:T(8,128)(2,1)S(1)} %pad_maximum_fusion.10), channel_id=1, source_target_pairs={{0,8},{4,12},{8,0},{12,4},{1,9},{5,13},{9,1},{13,5},{2,10},{6,14},... | collective-permute-start | bytes 98312 | tf_op jit(solution)/shard_map/ppermute | solution.py:15
  95.1 10.0 %collective-permute-start.15 = (bf16[128,128]{0,1:T(8,128)(2,1)S(1)}, bf16[128,128]{0,1:T(8,128)(2,1)S(1)}, u32[]{:S(2)}, u32[]{:S(2)}) collective-permute-start(bf16[128,128]{0,1:T(8,128)(2,1)S(1)} %pad_maximum_fusion.10), channel_id=1, source_target_pairs={{0,12},{4,8},{8,4},{12,0},{1,13},{5,9},{9,5},{13,1},{2,14},{6,10},... | collective-permute-start | bytes 98312 | tf_op jit(solution)/shard_map/ppermute | solution.py:15
  96.4 14.7 %collective-permute-start.19 = (bf16[2,4,64,2048]{3,2,1,0:T(8,128)(2,1)S(1)}, bf16[2,4,64,2048]{3,2,1,0:T(8,128)(2,1)S(1)}, u32[]{:S(2)}, u32[]{:S(2)}) collective-permute-start(bf16[2,4,64,2048]{3,2,1,0:T(8,128)(2,1)S(1)} %get-tuple-element.36), channel_id=1, source_target_pairs={{0,1},{1,0},{2,3},{3,2},{4,5},{5,4},{6,7},{7,6},{8,9},{9,8},{10,11... | collective-permute-start | bytes 6291464 | tf_op jit(solution)/shard_map/ppermute | solution.py:15
  106.0 2.7 %collective-permute-start.23 = (bf16[2,256,1024]{2,1,0:T(8,128)(2,1)S(1)}, bf16[2,256,1024]{2,1,0:T(8,128)(2,1)S(1)}, u32[]{:S(2)}, u32[]{:S(2)}) collective-permute-start(bf16[2,256,1024]{2,1,0:T(8,128)(2,1)S(1)} %bitcast.220), channel_id=1, source_target_pairs={{0,1},{1,0},{2,3},{3,2},{4,5},{5,4},{6,7},{7,6},{8,9},{9,8},{10,11... | collective-permute-start | bytes 3145736 | tf_op jit(solution)/shard_map/ppermute | solution.py:15
  107.5 2.8 %collective-permute-start.28 = (bf16[2,256,1024]{2,1,0:T(8,128)(2,1)S(1)}, bf16[2,256,1024]{2,1,0:T(8,128)(2,1)S(1)}, u32[]{:S(2)}, u32[]{:S(2)}) collective-permute-start(bf16[2,256,1024]{2,1,0:T(8,128)(2,1)S(1)} %bitcast.219), channel_id=1, source_target_pairs={{0,1},{1,0},{2,3},{3,2},{4,5},{5,4},{6,7},{7,6},{8,9},{9,8},{10,11... | collective-permute-start | bytes 3145736 | tf_op jit(solution)/shard_map/ppermute | solution.py:15
  108.3 29.6 %collective-permute-start.9 = (bf16[1,128,1024]{2,1,0:T(8,128)(2,1)S(1)}, bf16[1,128,1024]{2,1,0:T(8,128)(2,1)S(1)}, u32[]{:S(2)}, u32[]{:S(2)}) collective-permute-start(bf16[1,128,1024]{2,1,0:T(8,128)(2,1)S(1)} %fusion.36), channel_id=1, source_target_pairs={{0,8},{4,12},{8,0},{12,4},{1,9},{5,13},{9,1},{13,5},{2,10},{6,14},... | collective-permute-start | bytes 786440 | tf_op jit(solution)/shard_map/ppermute | solution.py:15
  109.5 16.0 %collective-permute-start.24 = (bf16[1,256,1024]{2,1,0:T(8,128)(2,1)S(1)}, bf16[1,256,1024]{2,1,0:T(8,128)(2,1)S(1)}, u32[]{:S(2)}, u32[]{:S(2)}) collective-permute-start(bf16[1,256,1024]{2,1,0:T(8,128)(2,1)S(1)} %fusion.26), channel_id=1, source_target_pairs={{0,2},{1,3},{2,0},{3,1},{4,6},{5,7},{6,4},{7,5},{8,10},{9,11},{10,... | collective-permute-start | bytes 1572872 | tf_op jit(solution)/shard_map/ppermute | solution.py:15
  112.9 4.7 %collective-permute-start.20 = (f32[128,64]{0,1:T(8,128)S(1)}, f32[128,64]{0,1:T(8,128)S(1)}, u32[]{:S(2)}, u32[]{:S(2)}) collective-permute-start(f32[128,64]{0,1:T(8,128)S(1)} %get-tuple-element.49), channel_id=1, source_target_pairs={{0,4},{4,0},{8,12},{12,8},{1,5},{5,1},{9,13},{13,9},{2,6},{6,2},{1... | collective-permute-start | bytes 98312 | tf_op jit(solution)/shard_map/ppermute | solution.py:15
  113.8 11.2 %collective-permute-start.21 = (f32[128,64]{0,1:T(8,128)S(1)}, f32[128,64]{0,1:T(8,128)S(1)}, u32[]{:S(2)}, u32[]{:S(2)}) collective-permute-start(f32[128,64]{0,1:T(8,128)S(1)} %get-tuple-element.51), channel_id=1, source_target_pairs={{0,8},{4,12},{8,0},{12,4},{1,9},{5,13},{9,1},{13,5},{2,10},{6,14},... | collective-permute-start | bytes 98312 | tf_op jit(solution)/shard_map/ppermute | solution.py:15
  115.8 9.1 %collective-permute-start.22 = (f32[128,64]{0,1:T(8,128)S(1)}, f32[128,64]{0,1:T(8,128)S(1)}, u32[]{:S(2)}, u32[]{:S(2)}) collective-permute-start(f32[128,64]{0,1:T(8,128)S(1)} %get-tuple-element.50), channel_id=1, source_target_pairs={{0,12},{4,8},{8,4},{12,0},{1,13},{5,9},{9,5},{13,1},{2,14},{6,10},... | collective-permute-start | bytes 98312 | tf_op jit(solution)/shard_map/ppermute | solution.py:15
  117.7 17.1 %collective-permute-start.29 = (bf16[1,256,1024]{2,1,0:T(8,128)(2,1)S(1)}, bf16[1,256,1024]{2,1,0:T(8,128)(2,1)S(1)}, u32[]{:S(2)}, u32[]{:S(2)}) collective-permute-start(bf16[1,256,1024]{2,1,0:T(8,128)(2,1)S(1)} %fusion.27), channel_id=1, source_target_pairs={{0,2},{1,3},{2,0},{3,1},{4,6},{5,7},{6,4},{7,5},{8,10},{9,11},{10,... | collective-permute-start | bytes 1572872 | tf_op jit(solution)/shard_map/ppermute | solution.py:15
  125.4 16.2 %collective-permute-start.33 = (bf16[2,256,1024]{2,1,0:T(8,128)(2,1)S(1)}, bf16[2,256,1024]{2,1,0:T(8,128)(2,1)S(1)}, u32[]{:S(2)}, u32[]{:S(2)}) collective-permute-start(bf16[2,256,1024]{2,1,0:T(8,128)(2,1)S(1)} %bitcast.195), channel_id=1, source_target_pairs={{0,1},{1,0},{2,3},{3,2},{4,5},{5,4},{6,7},{7,6},{8,9},{9,8},{10,11... | collective-permute-start | bytes 3145736 | tf_op jit(solution)/shard_map/ppermute | solution.py:15
  125.7 14.4 %collective-permute-start.25 = (bf16[64,1024]{1,0:T(8,128)(2,1)S(1)}, bf16[64,1024]{1,0:T(8,128)(2,1)S(1)}, u32[]{:S(2)}, u32[]{:S(2)}) collective-permute-start(bf16[64,1024]{1,0:T(8,128)(2,1)S(1)} %get-tuple-element.46), channel_id=1, source_target_pairs={{0,4},{4,0},{8,12},{12,8},{1,5},{5,1},{9,13},{13,9},{2,6},{6,2},{1... | collective-permute-start | bytes 393224 | tf_op jit(solution)/shard_map/ppermute | solution.py:15
  127.0 17.2 %collective-permute-start.26 = (bf16[64,1024]{1,0:T(8,128)(2,1)S(1)}, bf16[64,1024]{1,0:T(8,128)(2,1)S(1)}, u32[]{:S(2)}, u32[]{:S(2)}) collective-permute-start(bf16[64,1024]{1,0:T(8,128)(2,1)S(1)} %get-tuple-element.45), channel_id=1, source_target_pairs={{0,8},{4,12},{8,0},{12,4},{1,9},{5,13},{9,1},{13,5},{2,10},{6,14},... | collective-permute-start | bytes 393224 | tf_op jit(solution)/shard_map/ppermute | solution.py:15
  134.8 10.0 %collective-permute-start.27 = (bf16[64,1024]{1,0:T(8,128)(2,1)S(1)}, bf16[64,1024]{1,0:T(8,128)(2,1)S(1)}, u32[]{:S(2)}, u32[]{:S(2)}) collective-permute-start(bf16[64,1024]{1,0:T(8,128)(2,1)S(1)} %get-tuple-element.44), channel_id=1, source_target_pairs={{0,12},{4,8},{8,4},{12,0},{1,13},{5,9},{9,5},{13,1},{2,14},{6,10},... | collective-permute-start | bytes 393224 | tf_op jit(solution)/shard_map/ppermute | solution.py:15
  137.8 20.5 %collective-permute-start.30 = (bf16[64,1024]{1,0:T(8,128)(2,1)}, bf16[64,1024]{1,0:T(8,128)(2,1)S(1)}, u32[]{:S(2)}, u32[]{:S(2)}) collective-permute-start(bf16[64,1024]{1,0:T(8,128)(2,1)} %get-tuple-element.43), channel_id=1, source_target_pairs={{0,4},{4,0},{8,12},{12,8},{1,5},{5,1},{9,13},{13,9},{2,6},{6,2},{1... | collective-permute-start | bytes 393224 | tf_op jit(solution)/shard_map/ppermute | solution.py:15
  140.1 3.9 %copy-start.4 = (bf16[64,1024]{1,0:T(8,128)(2,1)}, bf16[64,1024]{1,0:T(8,128)(2,1)S(1)}, u32[]{:S(2)}) copy-start(bf16[64,1024]{1,0:T(8,128)(2,1)S(1)} %collective-permute-done.25.refs_0_) | copy-start | bytes 393220
  140.1 18.2 %collective-permute-start.31 = (bf16[64,1024]{1,0:T(8,128)(2,1)}, bf16[64,1024]{1,0:T(8,128)(2,1)}, u32[]{:S(2)}, u32[]{:S(2)}) collective-permute-start(bf16[64,1024]{1,0:T(8,128)(2,1)} %get-tuple-element.42), channel_id=1, source_target_pairs={{0,8},{4,12},{8,0},{12,4},{1,9},{5,13},{9,1},{13,5},{2,10},{6,14},... | collective-permute-start | bytes 393224 | tf_op jit(solution)/shard_map/ppermute | solution.py:15
  141.6 25.0 %collective-permute-start.32 = (bf16[64,1024]{1,0:T(8,128)(2,1)}, bf16[64,1024]{1,0:T(8,128)(2,1)}, u32[]{:S(2)}, u32[]{:S(2)}) collective-permute-start(bf16[64,1024]{1,0:T(8,128)(2,1)} %get-tuple-element.41), channel_id=1, source_target_pairs={{0,12},{4,8},{8,4},{12,0},{1,13},{5,9},{9,5},{13,1},{2,14},{6,10},... | collective-permute-start | bytes 393224 | tf_op jit(solution)/shard_map/ppermute | solution.py:15
  144.2 11.6 %collective-permute-start.34 = (bf16[1,256,1024]{2,1,0:T(8,128)(2,1)S(1)}, bf16[1,256,1024]{2,1,0:T(8,128)(2,1)S(1)}, u32[]{:S(2)}, u32[]{:S(2)}) collective-permute-start(bf16[1,256,1024]{2,1,0:T(8,128)(2,1)S(1)} %fusion.28), channel_id=1, source_target_pairs={{0,2},{1,3},{2,0},{3,1},{4,6},{5,7},{6,4},{7,5},{8,10},{9,11},{10,... | collective-permute-start | bytes 1572872 | tf_op jit(solution)/shard_map/ppermute | solution.py:15
  158.3 7.3 %collective-permute-start.35 = (bf16[2,64,1024]{2,1,0:T(8,128)(2,1)}, bf16[2,64,1024]{2,1,0:T(8,128)(2,1)S(1)}, u32[]{:S(2)}, u32[]{:S(2)}) collective-permute-start(bf16[2,64,1024]{2,1,0:T(8,128)(2,1)} %bitcast.211), channel_id=1, source_target_pairs={{0,4},{4,0},{8,12},{12,8},{1,5},{5,1},{9,13},{13,9},{2,6},{6,2},{1... | collective-permute-start | bytes 786440 | tf_op jit(solution)/shard_map/ppermute | solution.py:15
  165.7 6.3 %collective-permute-start.36 = (bf16[1,64,1024]{2,1,0:T(8,128)(2,1)S(1)}, bf16[1,64,1024]{2,1,0:T(8,128)(2,1)S(1)}, u32[]{:S(2)}, u32[]{:S(2)}) collective-permute-start(bf16[1,64,1024]{2,1,0:T(8,128)(2,1)S(1)} %fusion.44), channel_id=1, source_target_pairs={{0,8},{4,12},{8,0},{12,4},{1,9},{5,13},{9,1},{13,5},{2,10},{6,14},... | collective-permute-start | bytes 393224 | tf_op jit(solution)/shard_map/ppermute | solution.py:15
  167.5 5.3 %copy-start.1 = (f32[64,8192]{1,0:T(8,128)}, f32[64,8192]{1,0:T(8,128)S(1)}, u32[]{:S(2)}) copy-start(f32[64,8192]{1,0:T(8,128)S(1)} %convert_dynamic-update-slice_fusion) | copy-start | bytes 6291460
